TPU v7x, 32 devices: a whole 2x2x4 slice. The times are simulated.
32 devices in a mesh: bin: 16 (over z, x, core), diag: 2 (over y).
Axes of the slice: x: 2, y: 2, z: 4, core: 2. Of those that a mesh axis runs over, the one named last changes fastest.
Arguments:
- embeddings: bfloat16 [256, 6144], P('diag', 'bin'), may hold values from -6 to 6
- projection: bfloat16 [256, 64], P('diag'), may hold values from -0.375 to 0.375
- dist_bias: float32 [32, 256], replicated, may hold values from -3 to 3
- conv_weight: bfloat16 [2, 9, 32, 32], replicated, may hold values from -0.375 to 0.375
- head_weight: float32 [32], replicated, may hold values from -1 to 1
- dilations: int32 [2], replicated, may hold values from 1 to 4, as said below
- band_limit: int32 [6144], P('bin'), may hold values from 64 to 256
- cotangent: float32 [256, 6144], P('diag', 'bin'), may hold values from -6 to 6
Outputs:
- predicted: float32 [256, 6144], P('diag', 'bin')
- grad_embed: float32 [256, 6144], P('diag', 'bin')
- grad_proj: float32 [256, 64], P('diag')
- grad_conv: float32 [2, 9, 32, 32], replicated
Inputs may be any that keep to these rules, and one draw needn't show every extreme that they name: `dilations`: one of the 2 layers has dilation exactly 4.
All inputs are finite; a program needn't handle non-finite values.
Results may differ from a plain program's by a relative error of at most 0.0059.
Values may be sent and summed in bfloat16 or wider, within the bound.
A program may use at most 256 MiB of HBM per device.

v0:
```python
import math

import jax
import jax.numpy as jnp
from jax import lax
from jax.sharding import PartitionSpec as P

MAXDIL = 4


HIGHEST = lax.Precision.HIGHEST


def with_halo(block, sides, width):
    for axis, dim in sides:
        count = lax.axis_size(axis)
        forward = [(i, i + 1) for i in range(count - 1)]
        backward = [(target, source) for source, target in forward]
        low = lax.ppermute(
            lax.slice_in_dim(block, block.shape[dim] - width, None, axis=dim), axis, forward
        )
        high = lax.ppermute(lax.slice_in_dim(block, 0, width, axis=dim), axis, backward)
        block = jnp.concatenate([low, block, high], axis=dim)
    return block


def from_behind(x, axis, by):
    size = lax.axis_size(axis)
    pairs = [(i, i + by) for i in range(size) if 0 <= i + by < size]
    return lax.ppermute(x, axis, pairs)


def skew_read(window, diag_count, row_count):
    channels = window.shape[0]
    span_len = row_count + diag_count - 1
    tiled_rows = jnp.broadcast_to(window[:, None, :], (channels, diag_count, span_len)).reshape(
        channels, diag_count * span_len
    )
    tiled_rows = jnp.pad(tiled_rows, ((0, 0), (0, diag_count)))
    return tiled_rows.reshape(channels, diag_count, span_len + 1)[:, :, :row_count]


def skew_write(values):
    channels, diag_count, row_count = values.shape
    span_len = row_count + diag_count - 1
    padded = jnp.pad(values, ((0, 0), (0, 0), (0, span_len + 1 - row_count)))
    flat_view = padded.reshape(channels, diag_count * (span_len + 1))[:, : diag_count * span_len]
    return jnp.sum(flat_view.reshape(channels, diag_count, span_len), axis=1)


def tap_slice(padded, diag_start, row_start, diag_count, row_count):
    return lax.dynamic_slice(
        padded, (0, diag_start, row_start), (padded.shape[0], diag_count, row_count)
    )


def stacked_taps(padded, dilation, diag_count, row_count, sign):
    pieces = []
    for kernel_tap in range(9):
        along_bin = kernel_tap // 3 - 1
        along_diag = kernel_tap % 3 - 1
        pieces.append(
            tap_slice(
                padded,
                MAXDIL + sign * along_diag * dilation,
                MAXDIL + sign * along_bin * dilation,
                diag_count,
                row_count,
            )
        )
    return jnp.concatenate(pieces, axis=0)


def conv_forward(padded, weight, dilation, diag_count, row_count):
    outputs = weight.shape[1]
    flat_weight = jnp.transpose(weight, (1, 0, 2)).reshape(outputs, 9 * weight.shape[2])
    stacked = stacked_taps(padded, dilation, diag_count, row_count, 1)
    return jnp.einsum("ok,kdi->odi", flat_weight, stacked, preferred_element_type=jnp.float32)


def conv_transpose(padded, weight, dilation, diag_count, row_count):
    inputs = weight.shape[2]
    flat_weight = jnp.transpose(weight, (2, 0, 1)).reshape(inputs, 9 * weight.shape[1])
    stacked = stacked_taps(padded, dilation, diag_count, row_count, -1)
    return jnp.einsum("ck,kdi->cdi", flat_weight, stacked, preferred_element_type=jnp.float32)


def weight_grad(grad_values, padded, dilation, diag_count, row_count):
    outputs = grad_values.shape[0]
    inputs = padded.shape[0]
    stacked = stacked_taps(padded, dilation, diag_count, row_count, 1)
    product = jnp.einsum("odi,kdi->ok", grad_values, stacked, preferred_element_type=jnp.float32)
    return jnp.transpose(product.reshape(outputs, 9, inputs), (1, 0, 2))


def widen_band(values):
    return with_halo(values, (("bin", 2), ("diag", 1)), MAXDIL)


def on_device(
    embeddings, projection, dist_bias, conv_weight, head_weight, dilations, band_limit, cotangent
):
    channels = conv_weight.shape[2]
    diag_dev = cotangent.shape[0]
    rows_dev = cotangent.shape[1]
    margin = MAXDIL
    total_bins = rows_dev * lax.axis_size("bin")
    total_diags = diag_dev * lax.axis_size("diag")
    first_row = lax.axis_index("bin") * rows_dev
    first_diag = lax.axis_index("diag") * diag_dev
    dilation_one = dilations[0]
    dilation_two = dilations[1]
    projected = lax.psum(
        jnp.einsum("ek,eb->kb", projection, embeddings, preferred_element_type=jnp.float32), "diag"
    )
    left_proj = projected[:channels]
    right_proj = projected[channels:]
    right_next = from_behind(right_proj, "bin", -1)
    right_both = jnp.concatenate([right_proj, right_next], axis=1)
    bias_padded = jnp.pad(dist_bias, ((0, 0), (margin, margin)))
    row_ids = first_row + jnp.arange(rows_dev, dtype=jnp.int32)[None, :]
    diag_ids = first_diag + jnp.arange(diag_dev, dtype=jnp.int32)[:, None]
    inside = row_ids + diag_ids < total_bins
    inside_mask = inside.astype(jnp.float32)
    counted_mask = (inside & (diag_ids < band_limit[None, :])).astype(jnp.float32)
    window = lax.dynamic_slice_in_dim(right_both, first_diag, rows_dev + diag_dev - 1, 1)
    bias_cols = lax.dynamic_slice_in_dim(bias_padded, first_diag + margin, diag_dev, 1)
    tanh_zero = jnp.tanh(
        left_proj[:, None, :] + skew_read(window, diag_dev, rows_dev) + bias_cols[:, :, None]
    )
    pair_zero = (inside_mask * tanh_zero).astype(jnp.bfloat16)
    padded_zero = with_halo(pair_zero, (("bin", 2), ("diag", 1)), margin)
    act_one = conv_forward(padded_zero, conv_weight[0], dilation_one, diag_dev, rows_dev)
    tanh_one = jnp.tanh(act_one)
    pair_one = (inside_mask * (pair_zero.astype(jnp.float32) + tanh_one)).astype(jnp.bfloat16)
    padded_one = widen_band(pair_one)
    tanh_two = jnp.tanh(conv_forward(padded_one, conv_weight[1], dilation_two, diag_dev, rows_dev))
    pred_local = counted_mask * jnp.einsum("c,cdi->di", head_weight, tanh_two, precision=HIGHEST)
    grad_two = (
        (cotangent * counted_mask)[None, :, :]
        * head_weight[:, None, None]
        * (1.0 - tanh_two * tanh_two)
    ).astype(jnp.bfloat16)
    wgrad_two = weight_grad(grad_two, padded_one, dilation_two, diag_dev, rows_dev)
    back_one = conv_transpose(
        widen_band(grad_two), conv_weight[1], dilation_two, diag_dev, rows_dev
    )
    grad_one = (back_one * inside_mask * (1.0 - tanh_one * tanh_one)).astype(jnp.bfloat16)
    wgrad_one = weight_grad(grad_one, padded_zero, dilation_one, diag_dev, rows_dev)
    back_zero = inside_mask * back_one + conv_transpose(
        widen_band(grad_one), conv_weight[0], dilation_one, diag_dev, rows_dev
    )
    grad_pre = back_zero * inside_mask * (1.0 - tanh_zero * tanh_zero)
    left_local = jnp.sum(grad_pre, axis=1)
    spilled = skew_write(grad_pre)
    buffer = lax.dynamic_update_slice_in_dim(
        jnp.zeros((channels, 2 * rows_dev), jnp.float32), spilled, first_diag, 1
    )
    incoming = from_behind(buffer[:, rows_dev:].astype(jnp.bfloat16), "bin", 1).astype(jnp.float32)
    grad_right = buffer[:, :rows_dev] + incoming
    grad_both = lax.psum(jnp.concatenate([left_local, grad_right], axis=0), "diag")
    grad_embed = jnp.einsum(
        "ek,kb->eb", projection.astype(jnp.float32), grad_both, precision=HIGHEST
    )
    proj_part = jnp.einsum(
        "eb,kb->ek", embeddings.astype(jnp.float32), grad_both, precision=HIGHEST
    )
    conv_part = jnp.stack([wgrad_one, wgrad_two])
    conv_sum = lax.psum(conv_part, ("bin", "diag"))
    proj_sum = lax.psum(proj_part, "bin")
    scaling = 1.0 / math.sqrt(total_bins * total_diags)
    return (pred_local, grad_embed, scaling * proj_sum, scaling * conv_sum)


def solution(mesh):
    return jax.shard_map(
        on_device,
        mesh=mesh,
        in_specs=(
            P("diag", "bin"),
            P("diag", None),
            P(),
            P(),
            P(),
            P(),
            P("bin"),
            P("diag", "bin"),
        ),
        out_specs=(P("diag", "bin"), P("diag", "bin"), P("diag", None), P()),
        check_vma=False,
    )
```

profile of v0, /device:TPU:0, one launch (start us, length us, event | category | flops | bytes accessed | tf_op | source)
XLA Modules:
  0.0 700.4 jit_solution(18200268497774056696)
XLA Ops:
  10.4 24.2 %all-reduce.7.cloned.1.call-done = f32[64,384]{1,0:T(8,128)} async-done(((f32[64,384]{1,0:T(8,128)}), f32[64,384]{1,0:T(8,128)}) %all-reduce.7.cloned.1.call-update) | async-done | bytes 98320 | tf_op jit(solution)/shard_map/psum | solution.py:113
  38.6 4.4 broadcast_in_dim.4
  43.0 9.2 %reshape.111 = f32[32,65408]{1,0:T(8,128)} reshape(f32[32,128,511]{2,1,0:T(8,128)} %broadcast_in_dim.4) | data formatting | bytes 16744448 | tf_op jit(solution)/shard_map/reshape | solution.py:36
  52.3 3.9 pad.12
  56.2 4.9 copy.77
  61.9 4.0 multiply_convert_fusion
  71.1 4.9 collective-permute-start.1
  101.9 4.1 pad_maximum_fusion
  109.1 3.7 dynamic-slice_dynamic-update-slice_fusion.30
  112.7 3.6 dynamic-slice_dynamic-update-slice_fusion.29
  116.3 3.6 dynamic-slice_dynamic-update-slice_fusion.28
  119.9 16.7 %constant_dynamic-update-slice_fusion = bf16[288,128,384]{2,0,1:T(8,128)(2,1)} fusion(bf16[288,128,384]{2,0,1:T(8,128)(2,1)} %dynamic-slice_dynamic-update-slice_fusion.28, f32[32,128]{0,1:T(8,128)S(1)} %copy.34, f32[32,128,384]{2,1,0:T(8,128)S(1)} %bitcast.118, f32[32,384]{1,0:T(8,128)S(1)} %get-tuple-element.36, f32[128,384]{1,0:T(8,128)S(1)} %fusion.14), kind=kLoop, calls=%fused_computation.81 | loop fusion | flops 6291456 | bytes 9699328
  140.1 3.6 dynamic-slice_dynamic-update-slice_fusion.26
  143.7 3.5 dynamic-slice_dynamic-update-slice_fusion.25
  147.2 3.5 dynamic-slice_dynamic-update-slice_fusion.24
  150.7 14.1 %fusion.11 = (bf16[32,128,384]{2,0,1:T(8,128)(2,1)S(1)}, f32[128,384,32]{1,2,0:T(8,128)}) fusion(bf16[32,128,384]{2,0,1:T(8,128)(2,1)S(1)} %copy-done.6, f32[128,384]{1,0:T(8,128)S(1)} %fusion.14, bf16[288,128,384]{2,0,1:T(8,128)(2,1)} %dynamic-slice_dynamic-update-slice_fusion.24, bf16[32,288,1]{0,1,2:T(8,128)(2,1)S(1)} %bitcast.129), kind=kOutput, calls=%fused_computation.17 | convolution fusion | flops 912261120 | bytes 41109504 | tf_op jit(solution)/shard_map/ok,kdi->odi/dot_general | solution.py:78
  185.3 4.2 collective-permute-start.7
  197.4 5.0 pad_maximum_fusion.1
  220.6 9.3 %copy-done.1 = bf16[288,128,384]{2,0,1:T(8,128)(2,1)} copy-done((bf16[288,128,384]{2,0,1:T(8,128)(2,1)}, bf16[288,128,384]{2,0,1:T(8,128)(2,1)S(1)}, u32[]{:S(2)}) %copy-start.1) | copy-done | bytes 28311576
  230.0 11.7 %fusion.28 = f32[128,384,32]{1,2,0:T(8,128)S(1)} fusion(bf16[288,128,384]{2,0,1:T(8,128)(2,1)} %copy-done.1, bf16[32,288,1]{0,1,2:T(8,128)(2,1)S(1)} %bitcast.130), kind=kOutput, calls=%fused_computation.104 | convolution fusion | flops 905969664 | bytes 34621440 | tf_op jit(solution)/shard_map/ok,kdi->odi/dot_general | solution.py:78
  241.8 3.7 fusion.5
  272.9 4.7 collective-permute-done.12
  277.6 4.5 pad_maximum_fusion.2
  285.0 3.6 dynamic-slice_dynamic-update-slice_fusion.14
  292.1 3.6 dynamic-slice_dynamic-update-slice_fusion.12
  298.9 3.6 dynamic-slice_dynamic-update-slice_fusion.11
  302.4 3.6 dynamic-slice_dynamic-update-slice_fusion.10
  306.0 3.8 dynamic-slice_dynamic-update-slice_fusion.9
  309.8 3.6 dynamic-slice_dynamic-update-slice_fusion.8
  313.4 16.5 %fusion.4 = (bf16[32,128,384]{2,0,1:T(8,128)(2,1)S(1)}, f32[128,384,32]{1,2,0:T(8,128)}) fusion(f32[128,384,32]{1,2,0:T(8,128)} %get-tuple-element.43, f32[128,384]{1,0:T(8,128)S(1)} %fusion.14, bf16[288,128,384]{2,0,1:T(8,128)(2,1)} %dynamic-slice_dynamic-update-slice_fusion.8, bf16[32,288,1]{0,1,2:T(8,128)(2,1)S(1)} %bitcast.128), kind=kOutput, calls=%fused_computation.7 | convolution fusion | flops 913833984 | bytes 44255232 | tf_op jit(solution)/shard_map/ck,kdi->cdi/dot_general | solution.py:85
  342.7 14.4 %fusion.30 = f32[32,288,1]{0,1,2:T(8,128)} fusion(bf16[32,128,384]{2,0,1:T(8,128)(2,1)} %copy-done.7, bf16[288,128,384]{2,0,1:T(8,128)(2,1)} %copy-done.1), kind=kOutput, calls=%fused_computation.106 | convolution fusion | flops 905969664 | bytes 31494144 | tf_op jit(solution)/shard_map/odi,kdi->ok/dot_general | solution.py:92
  368.0 13.2 %fusion.29 = f32[32,288,1]{0,1,2:T(8,128)} fusion(bf16[32,128,384]{2,0,1:T(8,128)(2,1)S(1)} %get-tuple-element.44, bf16[288,128,384]{2,0,1:T(8,128)(2,1)} %dynamic-slice_dynamic-update-slice_fusion.24), kind=kOutput, calls=%fused_computation.105 | convolution fusion | flops 905969664 | bytes 31494144 | tf_op jit(solution)/shard_map/odi,kdi->ok/dot_general | solution.py:92
  387.4 3.5 dynamic-slice_dynamic-update-slice_fusion.6
  390.9 3.5 dynamic-slice_dynamic-update-slice_fusion.5
  394.4 3.6 dynamic-slice_dynamic-update-slice_fusion.4
  400.0 3.7 dynamic-slice_dynamic-update-slice_fusion.3
  403.7 3.5 dynamic-slice_dynamic-update-slice_fusion.2
  407.2 4.0 dynamic-slice_dynamic-update-slice_fusion.1
  414.7 20.0 %fusion.26 = (f32[32,384]{1,0:T(8,128)S(1)}, f32[32,128,384]{2,0,1:T(8,128)}) fusion(f32[32,128]{0,1:T(8,128)S(1)} %copy.34, f32[32,128,384]{2,1,0:T(8,128)} %copy-done.2, f32[32,384]{1,0:T(8,128)S(1)} %get-tuple-element.36, f32[128,384]{1,0:T(8,128)S(1)} %fusion.14, bf16[288,128,384]{2,0,1:T(8,128)(2,1)} %dynamic-slice_dynamic-update-slice_fusion, ...), kind=kOutput, calls=%fused_computation.102 | convolution fusion | flops 920113152 | bytes 47515648 | tf_op jit(solution)/shard_map/ck,kdi->cdi/dot_general | solution.py:85
  434.8 6.4 copy.76
  442.4 4.9 copy.78
  447.2 3.8 slice.118
  451.1 10.8 %reshape.118 = f32[32,128,511]{2,1,0:T(8,128)} reshape(f32[32,65408]{1,0:T(8,128)} %slice.118) | data formatting | bytes 16744448 | tf_op jit(solution)/shard_map/reshape | solution.py:48
  461.9 4.6 reduce_sum.19
  467.1 4.0 collective-permute-start.17
  472.7 131.4 %all-reduce.11.cloned.1.call-done = f32[2,9,32,32]{2,3,1,0:T(8,128)} async-done(((f32[2,9,32,32]{2,3,1,0:T(8,128)}), f32[2,9,32,32]{2,3,1,0:T(8,128)}) %all-reduce.11.cloned.1.call-update) | async-done | bytes 73744 | tf_op jit(solution)/shard_map/psum | solution.py:169
  606.0 23.1 %all-reduce.9.cloned.1.call-done = f32[64,384]{1,0:T(8,128)} async-done(((f32[64,384]{1,0:T(8,128)}), f32[64,384]{1,0:T(8,128)}) %all-reduce.9.cloned.1.call-update) | async-done | bytes 98320 | tf_op jit(solution)/shard_map/psum | solution.py:161
  632.2 60.8 %psum.30 = f32[128,64]{0,1:T(8,128)S(1)} all-reduce(f32[128,64]{0,1:T(8,128)S(1)} %convolution_bitcast_fusion.1), channel_id=1, replica_groups=mesh['bin'=16,'diag'=2] {'bin'}, use_global_device_ids=true, to_apply=%region_4.5 | all-reduce | flops 8192 | bytes 65536 | tf_op jit(solution)/shard_map/psum | solution.py:170
  (169 shorter events, 167.8 us)
Async XLA Ops:
  7.2 27.4 %all-reduce.7.cloned.1.call-start = ((), (), s32[]{:S(2)}) async-start(), calls=%async_computation | async-start | bytes 196608 | tf_op jit(solution)/shard_map/psum | solution.py:113
  9.6 594.5 %all-reduce.11.cloned.1.call-start = ((), (), s32[]{:S(2)}) async-start(), calls=%async_computation.2 | async-start | bytes 589824 | tf_op jit(solution)/shard_map/psum | solution.py:169
  35.4 3.1 collective-permute-start
  61.9 6.2 copy-start.2
  65.9 36.0 %copy-start.5 = (bf16[32,128,384]{2,0,1:T(8,128)(2,1)}, bf16[32,128,384]{2,0,1:T(8,128)(2,1)S(1)}, u32[]{:S(2)}) copy-start(bf16[32,128,384]{2,0,1:T(8,128)(2,1)S(1)} %multiply_convert_fusion) | copy-start | bytes 9437188
  71.1 10.9 %collective-permute-start.1 = (bf16[32,128,4]{1,0,2:T(8,128)(2,1)}, bf16[32,128,4]{1,0,2:T(8,128)(2,1)}, u32[]{:S(2)}, u32[]{:S(2)}) collective-permute-start(bf16[32,128,4]{1,0,2:T(8,128)(2,1)} %copy.35), channel_id=1, source_target_pairs={{0,2},{2,4},{4,6},{6,8},{8,10},{10,12},{12,14},{14,16},{16,18},{18... | collective-permute-start | bytes 98312 | tf_op jit(solution)/shard_map/ppermute | solution.py:19
  79.0 6.3 collective-permute-start.2
  90.3 10.0 %collective-permute-start.3 = (bf16[32,4,392]{2,0,1:T(8,128)(2,1)}, bf16[32,4,392]{2,0,1:T(8,128)(2,1)}, u32[]{:S(2)}, u32[]{:S(2)}) collective-permute-start(bf16[32,4,392]{2,0,1:T(8,128)(2,1)} %get-tuple-element.22), channel_id=1, source_target_pairs={{0,1},{2,3},{4,5},{6,7},{8,9},{10,11},{12,13},{14,15},{16,17},{18,... | collective-permute-start | bytes 301064 | tf_op jit(solution)/shard_map/ppermute | solution.py:19
  93.4 8.4 %collective-permute-start.4 = (bf16[32,4,392]{2,0,1:T(8,128)(2,1)}, bf16[32,4,392]{2,0,1:T(8,128)(2,1)}, u32[]{:S(2)}, u32[]{:S(2)}) collective-permute-start(bf16[32,4,392]{2,0,1:T(8,128)(2,1)} %get-tuple-element.23), channel_id=1, source_target_pairs={{1,0},{3,2},{5,4},{7,6},{9,8},{11,10},{13,12},{15,14},{17,16},{19,... | collective-permute-start | bytes 301064 | tf_op jit(solution)/shard_map/ppermute | solution.py:22
  109.1 10.8 %slice-start = ((s8[6291456]{0:T(1024)(128)(4,1)}), s8[4194304]{0:T(1024)(128)(4,1)S(1)}, s32[]{:S(2)}) async-start(s8[6291456]{0:T(1024)(128)(4,1)} %bitcast.117), calls=%async_computation.3 | async-start | bytes 8388608
  112.7 7.2 %slice-start.1 = ((s8[6291456]{0:T(1024)(128)(4,1)}), s8[2097152]{0:T(1024)(128)(4,1)S(1)}, s32[]{:S(2)}) async-start(s8[6291456]{0:T(1024)(128)(4,1)} %bitcast.117), calls=%async_computation.4 | async-start | bytes 4194304
  143.7 7.1 %copy-start.6 = (bf16[32,128,384]{2,0,1:T(8,128)(2,1)S(1)}, bf16[32,128,384]{2,0,1:T(8,128)(2,1)}, u32[]{:S(2)}) copy-start(bf16[32,128,384]{2,0,1:T(8,128)(2,1)} %copy-done.5) | copy-start | bytes 9437188
  143.7 7.1 %copy-start.16 = (bf16[32,9,32]{0,2,1:T(8,128)(2,1)S(1)}, bf16[32,9,32]{0,2,1:T(8,128)(2,1)}, u32[]{:S(2)}) copy-start(bf16[32,9,32]{0,2,1:T(8,128)(2,1)} %copy.39) | copy-start | bytes 55300
  164.9 20.4 %copy-start.4 = (bf16[32,128,384]{2,0,1:T(8,128)(2,1)}, bf16[32,128,384]{2,0,1:T(8,128)(2,1)S(1)}, u32[]{:S(2)}) copy-start(bf16[32,128,384]{2,0,1:T(8,128)(2,1)S(1)} %get-tuple-element.42) | copy-start | bytes 9437188
  170.1 6.8 collective-permute-start.5
  175.6 4.6 collective-permute-start.6
  185.3 9.2 %collective-permute-start.7 = (bf16[32,4,392]{2,0,1:T(8,128)(2,1)}, bf16[32,4,392]{2,0,1:T(8,128)(2,1)S(1)}, u32[]{:S(2)}, u32[]{:S(2)}) collective-permute-start(bf16[32,4,392]{2,0,1:T(8,128)(2,1)} %get-tuple-element.20), channel_id=1, source_target_pairs={{0,1},{2,3},{4,5},{6,7},{8,9},{10,11},{12,13},{14,15},{16,17},{18,... | collective-permute-start | bytes 301064 | tf_op jit(solution)/shard_map/ppermute | solution.py:19
  189.5 7.9 %collective-permute-start.8 = (bf16[32,4,392]{2,0,1:T(8,128)(2,1)}, bf16[32,4,392]{2,0,1:T(8,128)(2,1)S(1)}, u32[]{:S(2)}, u32[]{:S(2)}) collective-permute-start(bf16[32,4,392]{2,0,1:T(8,128)(2,1)} %get-tuple-element.21), channel_id=1, source_target_pairs={{1,0},{3,2},{5,4},{7,6},{9,8},{11,10},{13,12},{15,14},{17,16},{19,... | collective-permute-start | bytes 301064 | tf_op jit(solution)/shard_map/ppermute | solution.py:22
  220.6 9.3 %copy-start.1 = (bf16[288,128,384]{2,0,1:T(8,128)(2,1)}, bf16[288,128,384]{2,0,1:T(8,128)(2,1)S(1)}, u32[]{:S(2)}) copy-start(bf16[288,128,384]{2,0,1:T(8,128)(2,1)S(1)} %dynamic-slice_dynamic-update-slice_fusion.16) | copy-start | bytes 84934656
  230.0 11.8 %copy-start.21 = (f32[32]{0:T(128)S(1)}, f32[32]{0:T(128)}, u32[]{:S(2)}) copy-start(f32[32]{0:T(128)} %param.12) | copy-start | bytes 388
  241.7 6.0 copy-start.3
  241.8 3.8 copy-start.17
  241.8 3.8 copy-start.20
  241.8 3.8 copy-start.23
  241.8 3.8 copy-start.25
  246.4 3.5 copy-start.10
  247.8 29.8 %copy-start.7 = (bf16[32,128,384]{2,0,1:T(8,128)(2,1)}, bf16[32,128,384]{2,0,1:T(8,128)(2,1)S(1)}, u32[]{:S(2)}) copy-start(bf16[32,128,384]{2,0,1:T(8,128)(2,1)S(1)} %fusion.9) | copy-start | bytes 9437188
  253.0 7.2 %collective-permute-start.9 = (bf16[32,128,4]{1,0,2:T(8,128)(2,1)}, bf16[32,128,4]{1,0,2:T(8,128)(2,1)}, u32[]{:S(2)}, u32[]{:S(2)}) collective-permute-start(bf16[32,128,4]{1,0,2:T(8,128)(2,1)} %copy.47), channel_id=1, source_target_pairs={{0,2},{2,4},{4,6},{6,8},{8,10},{10,12},{12,14},{14,16},{16,18},{18... | collective-permute-start | bytes 98312 | tf_op jit(solution)/shard_map/ppermute | solution.py:19
  258.9 5.0 collective-permute-start.10
  268.2 4.7 collective-permute-start.11
  270.4 7.2 %collective-permute-start.12 = (bf16[32,4,392]{2,0,1:T(8,128)(2,1)S(1)}, bf16[32,4,392]{2,0,1:T(8,128)(2,1)S(1)}, u32[]{:S(2)}, u32[]{:S(2)}) collective-permute-start(bf16[32,4,392]{2,0,1:T(8,128)(2,1)S(1)} %get-tuple-element.19), channel_id=1, source_target_pairs={{1,0},{3,2},{5,4},{7,6},{9,8},{11,10},{13,12},{15,14},{17,16},{19,... | collective-permute-start | bytes 301064 | tf_op jit(solution)/shard_map/ppermute | solution.py:22
  285.0 10.7 %slice-start.2 = ((s8[6291456]{0:T(1024)(128)(4,1)}), s8[4194304]{0:T(1024)(128)(4,1)S(1)}, s32[]{:S(2)}) async-start(s8[6291456]{0:T(1024)(128)(4,1)} %bitcast.119), calls=%async_computation.5 | async-start | bytes 8388608
  288.6 7.1 %slice-start.3 = ((s8[6291456]{0:T(1024)(128)(4,1)}), s8[2097152]{0:T(1024)(128)(4,1)S(1)}, s32[]{:S(2)}) async-start(s8[6291456]{0:T(1024)(128)(4,1)} %bitcast.119), calls=%async_computation.6 | async-start | bytes 4194304
  288.6 7.1 %copy-start.11 = (f32[128,384]{1,0:T(8,128)S(1)}, f32[128,384]{1,0:T(8,128)}, u32[]{:S(2)}) copy-start(f32[128,384]{1,0:T(8,128)} %copy-done.10) | copy-start | bytes 589828
  288.6 7.1 %copy-start.22 = (f32[32]{0:T(128)S(1)}, f32[32]{0:T(128)}, u32[]{:S(2)}) copy-start(f32[32]{0:T(128)} %param.12) | copy-start | bytes 388
  306.0 7.4 %copy-start.15 = (bf16[1,9,32,32]{3,2,1,0:T(8,128)(2,1)S(1)}, bf16[1,9,32,32]{3,2,1,0:T(8,128)(2,1)}, u32[]{:S(2)}) copy-start(bf16[1,9,32,32]{3,2,1,0:T(8,128)(2,1)} %get-tuple-element.35) | copy-start | bytes 55300
  334.9 22.2 %collective-permute-start.13 = (bf16[32,128,4]{1,0,2:T(8,128)(2,1)}, bf16[32,128,4]{1,0,2:T(8,128)(2,1)}, u32[]{:S(2)}, u32[]{:S(2)}) collective-permute-start(bf16[32,128,4]{1,0,2:T(8,128)(2,1)} %copy.52), channel_id=1, source_target_pairs={{0,2},{2,4},{4,6},{6,8},{8,10},{10,12},{12,14},{14,16},{16,18},{18... | collective-permute-start | bytes 98312 | tf_op jit(solution)/shard_map/ppermute | solution.py:19
  341.4 19.1 %collective-permute-start.14 = (bf16[32,128,4]{1,0,2:T(8,128)(2,1)}, bf16[32,128,4]{1,0,2:T(8,128)(2,1)}, u32[]{:S(2)}, u32[]{:S(2)}) collective-permute-start(bf16[32,128,4]{1,0,2:T(8,128)(2,1)} %copy.53), channel_id=1, source_target_pairs={{2,0},{4,2},{6,4},{8,6},{10,8},{12,10},{14,12},{16,14},{18,16},{20... | collective-permute-start | bytes 98312 | tf_op jit(solution)/shard_map/ppermute | solution.py:22
  364.8 16.4 %collective-permute-start.15 = (bf16[32,4,392]{2,0,1:T(8,128)(2,1)S(1)}, bf16[32,4,392]{2,0,1:T(8,128)(2,1)S(1)}, u32[]{:S(2)}, u32[]{:S(2)}) collective-permute-start(bf16[32,4,392]{2,0,1:T(8,128)(2,1)S(1)} %get-tuple-element.16), channel_id=1, source_target_pairs={{0,1},{2,3},{4,5},{6,7},{8,9},{10,11},{12,13},{14,15},{16,17},{18,... | collective-permute-start | bytes 301064 | tf_op jit(solution)/shard_map/ppermute | solution.py:19
  366.5 14.7 %copy-start.8 = (bf16[32,128,4]{2,0,1:T(8,128)(2,1)S(1)}, bf16[32,128,4]{2,0,1:T(8,128)(2,1)}, u32[]{:S(2)}) copy-start(bf16[32,128,4]{2,0,1:T(8,128)(2,1)} %copy.54) | copy-start | bytes 98308
  366.5 14.7 %copy-start.9 = (bf16[32,128,4]{2,0,1:T(8,128)(2,1)S(1)}, bf16[32,128,4]{2,0,1:T(8,128)(2,1)}, u32[]{:S(2)}) copy-start(bf16[32,128,4]{2,0,1:T(8,128)(2,1)} %copy.55) | copy-start | bytes 98308
  366.5 14.7 %collective-permute-start.16 = (bf16[32,4,392]{2,0,1:T(8,128)(2,1)S(1)}, bf16[32,4,392]{2,0,1:T(8,128)(2,1)S(1)}, u32[]{:S(2)}, u32[]{:S(2)}) collective-permute-start(bf16[32,4,392]{2,0,1:T(8,128)(2,1)S(1)} %get-tuple-element.17), channel_id=1, source_target_pairs={{1,0},{3,2},{5,4},{7,6},{9,8},{11,10},{13,12},{15,14},{17,16},{19,... | collective-permute-start | bytes 301064 | tf_op jit(solution)/shard_map/ppermute | solution.py:22
  407.2 7.5 %copy-start.14 = (bf16[1,9,32,32]{3,2,1,0:T(8,128)(2,1)S(1)}, bf16[1,9,32,32]{3,2,1,0:T(8,128)(2,1)}, u32[]{:S(2)}) copy-start(bf16[1,9,32,32]{3,2,1,0:T(8,128)(2,1)} %get-tuple-element.32) | copy-start | bytes 55300
  461.8 9.3 %copy-start.12 = (f32[32,288,1]{0,1,2:T(8,128)S(1)}, f32[32,288,1]{0,1,2:T(8,128)}, u32[]{:S(2)}) copy-start(f32[32,288,1]{0,1,2:T(8,128)} %fusion.30) | copy-start | bytes 110596
  461.8 9.3 %copy-start.13 = (f32[32,288,1]{0,1,2:T(8,128)S(1)}, f32[32,288,1]{0,1,2:T(8,128)}, u32[]{:S(2)}) copy-start(f32[32,288,1]{0,1,2:T(8,128)} %fusion.29) | copy-start | bytes 110596
  461.8 167.2 %copy-start.18 = (bf16[128,64]{0,1:T(8,128)(2,1)S(1)}, bf16[128,64]{0,1:T(8,128)(2,1)}, u32[]{:S(2)}) copy-start(bf16[128,64]{0,1:T(8,128)(2,1)} %param.9) | copy-start | bytes 49156
  467.1 4.9 collective-permute-start.17
  471.9 157.1 %all-reduce.9.cloned.1.call-start = ((), (), s32[]{:S(2)}) async-start(), calls=%async_computation.1 | async-start | bytes 196608 | tf_op jit(solution)/shard_map/psum | solution.py:161
  (3 other events, 2.2 us)
Sparse Core Ops, SparseCore 0:
  10.8 23.7 all-reduce.6
  472.0 132.0 all-reduce.10
  607.0 21.9 all-reduce.8
where the time goes:
time: 711 us; the launch traced here: 700 us
  local copies, waits for them, and re-layouts  235 us (33%)
  waiting for transfers between devices  190 us (27%)
  matrix products  97.7 us (14%)
  blocking collectives  60.8 us (9%)
  other arithmetic  55.7 us (8%)
  starting transfers between devices  40.8 us (6%)
  between operations  20 us (3%)
    psum x1, waiting for transfers between devices, on_device(): conv_sum = lax.psum(conv_part, ('bin', 'diag'))  131 us
    unnamed x95, local copies, waits for them, and re-layouts  121 us
    psum x1, blocking collectives, on_device(): proj_sum = lax.psum(proj_part, 'bin')  60.8 us
    dot_general x2, matrix products, conv_transpose(): jnp.einsum('ck,kdi->cdi', flat_weight, stacked, preferred_element_type=jn...  36.6 us
    dot_general x2, matrix products, weight_grad(): jnp.einsum('odi,kdi->ok', grad_values, stacked, preferred_element_type=jn...  27.6 us
    dot_general x2, matrix products, conv_forward(): jnp.einsum('ok,kdi->odi', flat_weight, stacked, preferred_element_type=jn...  25.9 us
    ppermute x8, starting transfers between devices, with_halo(): lax.ppermute(lax.slice_in_dim(block, block.shape[dim] - width, None, axis...  24.9 us
    psum x1, waiting for transfers between devices, on_device(): lax.psum(jnp.einsum('ek,eb->kb', projection, embeddings, preferred_elemen...  24.2 us
  transfers between devices with their start and end apart: 21, of which 9 were waited for; matrix products, arithmetic and copies ran while one was open for 9% of the time, Pallas kernels for 0%

commit v1 on v0

v1 whole, which is shorter than its diff:
```python
import functools
import math

import jax
import jax.numpy as jnp
from jax import lax
from jax.experimental import pallas as pl
from jax.experimental.pallas import tpu as pltpu
from jax.sharding import PartitionSpec as P

MAXDIL = 4
HALO = 4 * MAXDIL
PACK = 8


HIGHEST = lax.Precision.HIGHEST


def cut(rows, most):
    return max(n for n in range(1, most + 1) if rows % n == 0)


def kernel(
    plan, info, left, right, bias, mats, expand, head, cots, pred, grad_left, grad_right, wgrad,
    x0, h0, s0, x1, h1, s1, g2, hg2, b1, wacc,
):
    sub, groups, total, n1, n2, n3, n4 = plan
    lanes = 256
    first = info[2]
    dil_one, dil_two = info[0], info[1]
    g_ids = lax.broadcasted_iota(jnp.int32, (groups, lanes), 0)
    diag_ids = g_ids * PACK + lax.shift_right_logical(
        lax.broadcasted_iota(jnp.int32, (groups, lanes), 1), 5
    )

    def inside_rows(start, count):
        rows = first + start + lax.broadcasted_iota(jnp.int32, (count, 1, 1), 0)
        bound = jnp.where(rows >= 0, total - rows, 0)
        return (diag_ids[None] < bound).reshape(count * groups, lanes)

    def store(x_ref, h_ref, start, count, value):
        value = value.astype(jnp.bfloat16).astype(jnp.float32)
        x_ref[pl.ds(start, count)] = value.astype(jnp.bfloat16).reshape(count, groups, lanes)
        size = count * groups
        g_row = lax.broadcasted_iota(jnp.int32, (count, groups, 128), 1).reshape(size, 128)
        below = jnp.where(g_row == 0, 0.0, pltpu.roll(value[:, 128:], 1, 0))
        above = jnp.where(g_row == groups - 1, 0.0, pltpu.roll(value[:, :128], size - 1, 0))
        h_ref[pl.ds(start, count), :, :128] = below.astype(jnp.bfloat16).reshape(
            count, groups, 128
        )
        h_ref[pl.ds(start, count), :, 128:] = above.astype(jnp.bfloat16).reshape(
            count, groups, 128
        )

    def taps(x_ref, h_ref, start, count, step):
        pieces = []
        for along in (-1, 0, 1):
            at = start + along * step
            pieces.append(x_ref[pl.ds(at, count)].reshape(count * groups, lanes))
            pieces.append(h_ref[pl.ds(at, count)].reshape(count * groups, lanes))
        return jnp.concatenate(pieces, axis=1)

    def conv(x_ref, h_ref, mat, start, count, step):
        return jnp.dot(
            taps(x_ref, h_ref, start, count, step),
            mats[mat],
            preferred_element_type=jnp.float32,
        )

    n0 = 4

    @pl.loop(0, (sub + 2 * HALO) // n0)
    def _(block):
        start = block * n0
        rows = []
        for u in range(n0):
            at = start + u
            halves = []
            for half in range(2):
                partner = right[half, pl.ds(at, groups, stride=PACK), :]
                halves.append(partner + left[half, pl.ds(at, 1), :])
            rows.append(jnp.concatenate(halves, axis=1) + bias[...])
        t = jnp.tanh(jnp.concatenate(rows, axis=0))
        keep = inside_rows(start, n0)
        s0[pl.ds(start, n0)] = (
            jnp.where(keep, 1.0 - t * t, 0.0).astype(jnp.bfloat16).reshape(n0, groups, lanes)
        )
        store(x0, h0, start, n0, jnp.where(keep, t, 0.0))

    @pl.loop(0, (sub + 6 * MAXDIL) // n1)
    def _(block):
        start = MAXDIL + block * n1
        t = jnp.tanh(conv(x0, h0, 0, start, n1, dil_one))
        keep = inside_rows(start, n1)
        s1[pl.ds(start, n1)] = (
            jnp.where(keep, 1.0 - t * t, 0.0).astype(jnp.bfloat16).reshape(n1, groups, lanes)
        )
        before = x0[pl.ds(start, n1)].reshape(n1 * groups, lanes).astype(jnp.float32)
        store(x1, h1, start, n1, jnp.where(keep, before + t, 0.0))

    @pl.loop(0, (sub + 4 * MAXDIL) // n2)
    def _(block):
        start = 2 * MAXDIL + block * n2
        t = jnp.tanh(conv(x1, h1, 1, start, n2, dil_two))
        scored = lax.dot_general(
            head[...], t.astype(jnp.bfloat16), (((1,), (1,)), ((), ())),
            preferred_element_type=jnp.float32,
        )
        pred[block] = scored[:PACK] + scored[PACK:]
        factor = lax.dot_general(
            cots[block], expand[...], (((0,), (0,)), ((), ())),
            preferred_element_type=jnp.float32,
        )
        store(g2, hg2, start, n2, factor * (1.0 - t * t))

    def weight_grad(layer, g_ref, x_ref, h_ref, step):
        wacc[...] = jnp.zeros_like(wacc)

        @pl.loop(0, sub // n4)
        def _(block):
            start = HALO + block * n4
            wacc[...] += lax.dot_general(
                g_ref[pl.ds(start, n4)].reshape(n4 * groups, lanes),
                taps(x_ref, h_ref, start, n4, step),
                (((0,), (0,)), ((), ())),
                preferred_element_type=jnp.float32,
            )

        width = 2 * lanes
        out_diag = lax.shift_right_logical(
            lax.broadcasted_iota(jnp.int32, (lanes, width), 0), 5
        )
        slot = lax.shift_right_logical(lax.broadcasted_iota(jnp.int32, (lanes, width), 1), 5)
        in_diag = jnp.where(slot < 8, slot, jnp.where(slot < 12, slot - 12, slot - 4))
        fold = (
            lax.broadcasted_iota(jnp.int32, (width, 32), 0) & 31
            == lax.broadcasted_iota(jnp.int32, (width, 32), 1)
        ).astype(jnp.float32)
        for a in range(3):
            product = wacc[:, a * width : (a + 1) * width]
            for b in range(3):
                picked = jnp.where(in_diag == out_diag + (b - 1) * step, product, 0.0)
                total_rows = picked[:32]
                for d in range(1, PACK):
                    total_rows = total_rows + picked[32 * d : 32 * (d + 1)]
                wgrad[layer, 3 * a + b] = jnp.dot(
                    total_rows, fold, precision=HIGHEST, preferred_element_type=jnp.float32
                )

    weight_grad(1, g2, x1, h1, dil_two)

    @pl.loop(0, (sub + 2 * MAXDIL) // n3)
    def _(block):
        start = 3 * MAXDIL + block * n3
        back = conv(g2, hg2, 2, start, n3, dil_two)
        b1[pl.ds(start, n3)] = back.reshape(n3, groups, lanes)
        scale = s1[pl.ds(start, n3)].reshape(n3 * groups, lanes).astype(jnp.float32)
        store(x1, h1, start, n3, back * scale)

    weight_grad(0, x1, x0, h0, dil_one)
    grad_right[...] = jnp.zeros_like(grad_right)

    @pl.loop(0, sub // n4)
    def _(block):
        start = HALO + block * n4
        back = conv(x1, h1, 3, start, n4, dil_one)
        scale = s0[pl.ds(start, n4)].reshape(n4 * groups, lanes).astype(jnp.float32)
        grad = (back + b1[pl.ds(start, n4)].reshape(n4 * groups, lanes)) * scale
        grad_left[block] = jnp.sum(grad.reshape(n4, groups, lanes), axis=1)
        for u in range(n4):
            at = pl.ds(block * n4 + u, groups, stride=PACK)
            for half in range(2):
                piece = grad[u * groups : (u + 1) * groups, 128 * half : 128 * (half + 1)]
                grad_right[half, at, :] = grad_right[half, at, :] + piece


def tap_matrix(weight, dilation, sign):
    diags = jnp.array([0, 1, 2, 3, 4, 5, 6, 7, -4, -3, -2, -1, 8, 9, 10, 11], jnp.int32)
    outs, ins = weight.shape[1], weight.shape[2]
    weight = weight.reshape(3, 3, outs, ins)
    if sign < 0:
        weight = weight[::-1]
    total = jnp.zeros((3, 16, ins, PACK, outs), weight.dtype)
    for b in range(3):
        hit = diags[:, None] == jnp.arange(PACK)[None, :] + sign * (b - 1) * dilation
        spread = jnp.transpose(weight[:, b], (0, 2, 1))[:, None, :, None, :]
        total = jnp.where(hit[None, :, None, :, None], spread, total)
    return total.reshape(3 * 16 * ins, PACK * outs)


def split_two(x):
    high = x.astype(jnp.bfloat16)
    return high, (x - high.astype(jnp.float32)).astype(jnp.bfloat16)


def shifted(axis, size, by):
    return [(i, i + by) for i in range(size) if 0 <= i + by < size]


def on_device(
    embeddings, projection, dist_bias, conv_weight, head_weight, dilations, band_limit, cotangent
):
    channels = conv_weight.shape[2]
    diag_dev, rows_dev = cotangent.shape
    n_bin, n_diag = lax.axis_size("bin"), lax.axis_size("diag")
    total_bins, diags = rows_dev * n_bin, diag_dev * n_diag
    me = lax.axis_index("diag")
    first_row = lax.axis_index("bin") * rows_dev
    sub = rows_dev // n_diag
    groups = diags // PACK
    lanes = PACK * channels
    reach = HALO + diags

    def around(block, before, after):
        low = lax.ppermute(block[:, rows_dev - before :], "bin", shifted("bin", n_bin, 1))
        high = lax.ppermute(block[:, :after], "bin", shifted("bin", n_bin, -1))
        return jnp.concatenate([low, block, high], axis=1)

    def pairs(k):
        return [(i, (i + k) % n_diag) for i in range(n_diag)]

    wide = around(embeddings, HALO, reach)
    part = jnp.einsum("eb,ek->bk", wide, projection, preferred_element_type=jnp.float32)
    span = sub + HALO + reach
    projected = lax.dynamic_slice_in_dim(part, me * sub, span, 0)
    for k in range(1, n_diag):
        other = lax.rem(me + k, n_diag)
        projected = projected + lax.ppermute(
            lax.dynamic_slice_in_dim(part, other * sub, span, 0), "diag", pairs(k)
        )
    region = sub + 2 * HALO
    reads = region + PACK * (groups - 1)
    left = jnp.tile(projected[:region, :channels], (1, PACK))
    right = jnp.concatenate(
        [projected[d : d + reads, channels:] for d in range(PACK)], axis=1
    )
    halves = lambda x: jnp.stack([x[:, : lanes // 2], x[:, lanes // 2 :]])
    bias = jnp.transpose(dist_bias.reshape(channels, groups, PACK), (1, 2, 0)).reshape(
        groups, lanes
    )

    row_ids = first_row + jnp.arange(rows_dev, dtype=jnp.int32)[None, :]
    diag_ids = me * diag_dev + jnp.arange(diag_dev, dtype=jnp.int32)[:, None]
    counted = (row_ids + diag_ids < total_bins) & (diag_ids < band_limit[None, :])
    margin = 2 * MAXDIL
    cot_wide = around(jnp.where(counted, cotangent, 0.0), margin, margin)
    cot_span = sub + 2 * margin
    cot = jnp.zeros((n_diag, diag_dev, cot_span), jnp.float32)
    for k in range(n_diag):
        other = lax.rem(me + k, n_diag)
        piece = lax.dynamic_slice_in_dim(cot_wide, other * sub, cot_span, 1)
        if k:
            piece = lax.ppermute(piece, "diag", pairs(k))
        cot = lax.dynamic_update_index_in_dim(cot, piece, lax.rem(me - k + n_diag, n_diag), 0)
    n1 = cut(sub + 6 * MAXDIL, 24)
    n2 = cut(cot_span, 16)
    n3 = cut(sub + 2 * MAXDIL, 25)
    n4 = cut(sub, 24)
    blocks = cot_span // n2
    cot = jnp.transpose(cot.reshape(groups, PACK, blocks, n2), (2, 1, 3, 0)).reshape(
        blocks, PACK, n2 * groups
    )
    cot_high, cot_low = split_two(cot)
    head_high, head_low = split_two(head_weight)
    eye = jnp.eye(PACK, dtype=jnp.bfloat16)
    spread = lambda h: (eye[:, :, None] * h[None, None, :]).reshape(PACK, lanes)
    pad = jnp.zeros((PACK, lanes), jnp.bfloat16)
    cots = jnp.concatenate([cot_high, cot_low, cot_high, jnp.zeros_like(cot_high)], axis=1)
    expand = jnp.concatenate([spread(head_high), spread(head_high), spread(head_low), pad])
    head = jnp.concatenate([spread(head_high), spread(head_low)])
    mats = jnp.stack(
        [
            tap_matrix(conv_weight[0], dilations[0], 1),
            tap_matrix(conv_weight[1], dilations[1], 1),
            tap_matrix(jnp.transpose(conv_weight[1], (0, 2, 1)), dilations[1], -1),
            tap_matrix(jnp.transpose(conv_weight[0], (0, 2, 1)), dilations[0], -1),
        ]
    )
    info = jnp.concatenate([dilations, (first_row + me * sub - HALO)[None].astype(jnp.int32)])

    writes = sub + PACK * (groups - 1)
    vmem = pl.BlockSpec(memory_space=pltpu.VMEM)
    half_map = pltpu.VMEM((region, groups, lanes), jnp.bfloat16)
    pred, grad_left, grad_right, conv_part = pl.pallas_call(
        functools.partial(kernel, (sub, groups, total_bins, n1, n2, n3, n4)),
        out_shape=[
            jax.ShapeDtypeStruct((blocks, PACK, n2 * groups), jnp.float32),
            jax.ShapeDtypeStruct((sub // n4, n4, lanes), jnp.float32),
            jax.ShapeDtypeStruct((2, writes, lanes // 2), jnp.float32),
            jax.ShapeDtypeStruct(conv_weight.shape, jnp.float32),
        ],
        in_specs=[pl.BlockSpec(memory_space=pltpu.SMEM)] + [vmem] * 7,
        out_specs=[vmem] * 4,
        scratch_shapes=[half_map] * 8
        + [
            pltpu.VMEM((region, groups, lanes), jnp.float32),
            pltpu.VMEM((lanes, 6 * lanes), jnp.float32),
        ],
        compiler_params=pltpu.CompilerParams(vmem_limit_bytes=60 * 1024 * 1024),
        name="band",
    )(info, halves(left), halves(right), bias, mats, expand, head, cots)

    conv_sum = lax.psum(conv_part, ("bin", "diag"))

    grad_right = jnp.concatenate([grad_right[0], grad_right[1]], axis=1)
    spilled = jnp.zeros((sub + diags, channels), jnp.float32)
    for d in range(PACK):
        spilled = spilled + jnp.pad(
            grad_right[:, d * channels : (d + 1) * channels],
            ((d, sub + diags - writes - d), (0, 0)),
        )
    lefts = jnp.sum(grad_left.reshape(sub, PACK, channels), axis=1)
    own = jnp.concatenate([jnp.pad(lefts, ((0, diags), (0, 0))), spilled], axis=1)
    buffer = lax.dynamic_update_slice_in_dim(
        jnp.zeros((rows_dev + diags, 2 * channels), jnp.float32), own, me * sub, 0
    )
    both = buffer
    for k in range(1, n_diag):
        both = both + lax.ppermute(buffer, "diag", pairs(k))
    incoming = lax.ppermute(both[rows_dev:, channels:], "bin", shifted("bin", n_bin, 1))
    both = both[:rows_dev] + jnp.pad(incoming, ((0, rows_dev - diags), (channels, 0)))
    grad_embed = jnp.einsum(
        "ek,bk->eb", projection.astype(jnp.float32), both, precision=HIGHEST
    )
    proj_part = jnp.einsum(
        "eb,bk->ek", embeddings.astype(jnp.float32), both, precision=HIGHEST
    )
    proj_sum = lax.psum(proj_part, "bin")

    pred = jnp.transpose(pred.reshape(blocks, PACK, n2, groups), (3, 1, 0, 2)).reshape(
        diags, cot_span
    )[:, margin : margin + sub]
    pred_local = jnp.zeros((diag_dev, rows_dev), jnp.float32)
    for k in range(n_diag):
        other = lax.rem(me + k, n_diag)
        piece = lax.dynamic_slice_in_dim(pred, other * diag_dev, diag_dev, 0)
        if k:
            piece = lax.ppermute(piece, "diag", pairs(k))
        pred_local = lax.dynamic_update_slice_in_dim(
            pred_local, piece, lax.rem(me - k + n_diag, n_diag) * sub, 1
        )
    pred_local = jnp.where(counted, pred_local, 0.0)
    scaling = 1.0 / math.sqrt(total_bins * diags)
    return (pred_local, grad_embed, scaling * proj_sum, scaling * conv_sum)


def solution(mesh):
    return jax.shard_map(
        on_device,
        mesh=mesh,
        in_specs=(
            P("diag", "bin"),
            P("diag", None),
            P(),
            P(),
            P(),
            P(),
            P("bin"),
            P("diag", "bin"),
        ),
        out_specs=(P("diag", "bin"), P("diag", "bin"), P("diag", None), P()),
        check_vma=False,
    )
```

time: 711 us -> 345 us (0.49); the launches traced: 700 us -> 344 us
  local copies, waits for them, and re-layouts: 235 us -> 35.9 us
  matrix products: 97.7 us -> 1.89 us
  waiting for transfers between devices: 190 us -> 129 us
  Pallas kernels: 0 us -> 57.6 us
  other arithmetic: 55.7 us -> 24.1 us
  starting transfers between devices: 40.8 us -> 16.3 us
    unnamed x95 -> x34, local copies, waits for them, and re-layouts: 121 us -> 1.16 us
    dot_general x10 -> x3, matrix products: 97.7 us -> 1.89 us  [the longest x1 1.21 us: on_device(): jnp.einsum('eb,ek->bk', wide, projection, preferred_element_type=jnp.floa...]
    pallas_call x0 -> x1, Pallas kernels: none -> 57.6 us  [on_device(): pl.pallas_call(functools.partial(kernel, (sub, groups, total_bins, n1, n2...]
    psum x2 -> x0, waiting for transfers between devices: 47.3 us -> none  [the longest x1 24.2 us: on_device(): lax.psum(jnp.einsum('ek,eb->kb', projection, embeddings, preferred_elemen...]
    slice x18 -> x14, local copies, waits for them, and re-layouts: 41.3 us -> 5.8 us  [the longest x2 2.17 us: around(): block[:, rows_dev - before:]]
    ppermute x8 -> x0, local copies, waits for them, and re-layouts: 26.7 us -> none  [the longest x4 13.4 us: with_halo(): lax.ppermute(lax.slice_in_dim(block, block.shape[dim] - width, None, axis...]
    ppermute x18 -> x9, starting transfers between devices: 40.7 us -> 16.2 us  [the longest x2 8.13 us: around(): lax.ppermute(block[:, rows_dev - before:], 'bin', shifted('bin', n_bin, 1))]
    unnamed x4 -> x0, other arithmetic: 19.7 us -> none
  transfers between devices with their start and end apart: 21 -> 10, of which waited for: 9 -> 4; matrix products, arithmetic and copies ran while one was open for 9% -> 15% of each run, Pallas kernels for 0% -> 0%
where the time goes in v1:
time: 345 us; the launch traced here: 344 us
  waiting for transfers between devices  129 us (37%)
  blocking collectives  63.2 us (18%)
  Pallas kernels  57.6 us (17%)
  local copies, waits for them, and re-layouts  35.9 us (10%)
  other arithmetic  24.1 us (7%)
  starting transfers between devices  16.3 us (5%)
  between operations  15.9 us (5%)
    psum x1, waiting for transfers between devices, on_device(): conv_sum = lax.psum(conv_part, ('bin', 'diag'))  125 us
    psum x1, blocking collectives, on_device(): proj_sum = lax.psum(proj_part, 'bin')  63.2 us
    pallas_call x1, Pallas kernels, on_device(): pl.pallas_call(functools.partial(kernel, (sub, groups, total_bins, n1, n2...  57.6 us
    select_n x4, local copies, waits for them, and re-layouts, tap_matrix(): total = jnp.where(hit[None, :, None, :, None], spread, total)  17.3 us
    ppermute x2, starting transfers between devices, around(): lax.ppermute(block[:, rows_dev - before:], 'bin', shifted('bin', n_bin, 1))  8.13 us
  transfers between devices with their start and end apart: 10, of which 4 were waited for; matrix products, arithmetic and copies ran while one was open for 15% of the time, Pallas kernels for 0%

profile of v1, /device:TPU:0, one launch (start us, length us, event | category | flops | bytes accessed | tf_op | source)
XLA Modules:
  0.0 344.0 jit_solution(14055546095193301659)
XLA Ops:
  7.3 1.0 fusion.9
  8.3 0.7 fusion.18
  9.0 3.0 collective-permute-start.3
  12.0 1.3 collective-permute-start.4
  13.3 1.3 collective-permute-start.1
  14.6 1.5 slice.158
  16.1 5.1 %collective-permute-start = (bf16[128,16]{1,0:T(8,128)(2,1)}, bf16[128,16]{1,0:T(8,128)(2,1)S(1)}, u32[]{:S(2)}, u32[]{:S(2)}) collective-permute-start(bf16[128,16]{1,0:T(8,128)(2,1)} %slice.158), channel_id=1, source_target_pairs={{0,2},{2,4},{4,6},{6,8},{8,10},{10,12},{12,14},{14,16},{16,18},{18... | collective-permute-start | bytes 12296 | tf_op jit(solution)/shard_map/ppermute | solution.py:215
  21.2 1.3 fusion.23
  23.2 0.6 iota_add_fusion.1
  24.5 0.6 iota_add_fusion.3
  25.1 0.9 fusion.19
  26.7 0.7 broadcast_compare_fusion.1
  27.5 5.8 %select_select_fusion.3 = (bf16[3,16,32,8,32]{4,3,2,1,0:T(8,128)(2,1)}, bf16[3,16,32,8,32]{4,3,2,1,0:T(8,128)(2,1)S(1)}, bf16[3,16,32,8,32]{4,3,2,1,0:T(8,128)(2,1)}, bf16[3,16,32,8,32]{4,3,2,1,0:T(8,128)(2,1)}) fusion(pred[16,8]{1,0:T(8,128)(4,1)S(1)} %get-tuple-element.72, pred[16,8]{1,0:T(8,128)(4,1)S(1)} %get-tuple-element.71, ...), kind=kLoop, calls=%fused_computation.4 | loop fusion | flops 4718592 | bytes 3220096 | tf_op jit(solution)/shard_map/jit(_where)/select_n | solution.py:187
  33.2 4.8 %select_n.187 = bf16[1,1536,256]{2,1,0:T(8,128)(2,1)} reshape(bf16[3,16,32,8,32]{4,3,2,1,0:T(8,128)(2,1)} %get-tuple-element.60) | data formatting | bytes 1572864 | tf_op jit(solution)/shard_map/jit(_where)/select_n | solution.py:187
  38.0 4.8 %select_n.191 = bf16[1,1536,256]{2,1,0:T(8,128)(2,1)} reshape(bf16[3,16,32,8,32]{4,3,2,1,0:T(8,128)(2,1)} %get-tuple-element.67) | data formatting | bytes 1572864 | tf_op jit(solution)/shard_map/jit(_where)/select_n | solution.py:187
  42.8 4.8 %select_n.195 = bf16[1,1536,256]{2,1,0:T(8,128)(2,1)} reshape(bf16[3,16,32,8,32]{4,3,2,1,0:T(8,128)(2,1)} %get-tuple-element.66) | data formatting | bytes 1572864 | tf_op jit(solution)/shard_map/jit(_where)/select_n | solution.py:187
  47.7 2.9 select_n.199
  51.6 0.7 maximum_maximum_fusion.1.expand
  52.3 3.2 pad_maximum_fusion.mats
  55.5 0.7 pad_add_fusion.1.info
  56.3 0.7 reshape.670.bias
  57.0 1.0 pad_maximum_fusion.2
  58.1 1.6 collective-permute-start.5
  59.9 1.2 fusion
  61.7 2.1 collective-permute-done.5
  64.4 1.1 copy.39
  65.9 1.5 maximum_maximum_fusion.cots
  67.5 2.2 collective-permute-done.2
  69.7 1.0 dynamic-slice_add_fusion
  72.1 0.8 pad_maximum_fusion.1.right
  72.9 0.7 pad_maximum_fusion.3.left
  73.6 57.6 %band.1 = (f32[13,8,512]{2,1,0:T(8,128)}, f32[8,24,256]{2,1,0:T(8,128)}, f32[2,440,128]{2,1,0:T(8,128)}, f32[2,9,32,32]{3,2,1,0:T(8,128)}) custom-call(s32[3]{0:T(128)} %pad_add_fusion.1.info, f32[2,224,128]{2,1,0:T(8,128)} %pad_maximum_fusion.3.left, f32[2,472,128]{2,1,0:T(8,128)} %pad_maximum_fusion.1.right, f32[32,256]{1,0:T(8,128)} %reshape.670.bias, ...), custom_call_target="tpu_custom_call" | custom-call | tf_op jit(solution)/shard_map/band/pallas_call | solution.py:284
  131.1 1.1 slice_bitcast_fusion.1
  133.5 0.8 broadcast_in_dim.246
  134.2 0.8 fusion.7
  135.0 1.0 collective-permute-start.7
  136.1 1.2 reshape.675
  137.2 1.8 copy.40
  139.1 0.8 reshape.676
  140.1 1.1 collective-permute-start.6
  141.1 0.9 dynamic_update_slice.20
  142.0 124.7 %all-reduce.12.cloned.1.call-done = f32[2,9,32,32]{3,2,1,0:T(8,128)} async-done(((f32[2,9,32,32]{3,2,1,0:T(8,128)}), f32[2,9,32,32]{3,2,1,0:T(8,128)}) %all-reduce.12.cloned.1.call-update) | async-done | bytes 73744 | tf_op jit(solution)/shard_map/psum | solution.py:303
  266.7 1.7 broadcast_multiply_fusion
  268.4 0.8 dynamic_update_slice.21
  269.5 1.3 collective-permute-start.8
  270.8 0.8 fusion.8
  272.2 63.2 %psum.14 = f32[128,64]{0,1:T(8,128)S(1)} all-reduce(f32[128,64]{0,1:T(8,128)S(1)} %convolution_bitcast_fusion.1), channel_id=1, replica_groups=mesh['bin'=16,'diag'=2] {'bin'}, use_global_device_ids=true, to_apply=%region_1.2 | all-reduce | flops 8192 | bytes 65536 | tf_op jit(solution)/shard_map/psum | solution.py:328
  336.3 0.8 copy.41
  (97 shorter events, 8.1 us)
Async XLA Ops:
  7.2 52.7 %copy-start = (bf16[128,64]{0,1:T(8,128)(2,1)S(1)}, bf16[128,64]{0,1:T(8,128)(2,1)}, u32[]{:S(2)}) copy-start(bf16[128,64]{0,1:T(8,128)(2,1)} %param.13) | copy-start | bytes 49156
  7.2 259.5 %all-reduce.12.cloned.1.call-start = ((), (), s32[]{:S(2)}) async-start(), calls=%async_computation | async-start | bytes 589824 | tf_op jit(solution)/shard_map/psum | solution.py:303
  7.2 17.2 %copy-start.10 = (s32[128]{0:T(128)}, s32[128]{0:T(128)S(1)}, u32[]{:S(2)}) copy-start(s32[128]{0:T(128)S(1)} %iota_add_fusion.5) | copy-start | bytes 1540
  7.3 7.3 %copy-start.7 = (s32[384]{0:T(512)}, s32[384]{0:T(512)S(1)}, u32[]{:S(2)}) copy-start(s32[384]{0:T(512)S(1)} %iota_add_fusion) | copy-start | bytes 4612
  9.0 48.0 %collective-permute-start.3 = (f32[128,8]{1,0:T(8,128)}, f32[128,8]{1,0:T(8,128)}, u32[]{:S(2)}, u32[]{:S(2)}) collective-permute-start(f32[128,8]{1,0:T(8,128)} %get-tuple-element.44), channel_id=1, source_target_pairs={{0,2},{2,4},{4,6},{6,8},{8,10},{10,12},{12,14},{14,16},{16,18},{18... | collective-permute-start | bytes 12296 | tf_op jit(solution)/shard_map/ppermute | solution.py:215
  12.0 45.0 %collective-permute-start.4 = (f32[128,8]{1,0:T(8,128)}, f32[128,8]{1,0:T(8,128)}, u32[]{:S(2)}, u32[]{:S(2)}) collective-permute-start(f32[128,8]{1,0:T(8,128)} %get-tuple-element.45), channel_id=1, source_target_pairs={{2,0},{4,2},{6,4},{8,6},{10,8},{12,10},{14,12},{16,14},{18,16},{20... | collective-permute-start | bytes 12296 | tf_op jit(solution)/shard_map/ppermute | solution.py:216
  13.3 46.6 %collective-permute-start.1 = (bf16[128,272]{1,0:T(8,128)(2,1)}, bf16[128,272]{1,0:T(8,128)(2,1)}, u32[]{:S(2)}, u32[]{:S(2)}) collective-permute-start(bf16[128,272]{1,0:T(8,128)(2,1)} %bitcast.108), channel_id=1, source_target_pairs={{2,0},{4,2},{6,4},{8,6},{10,8},{12,10},{14,12},{16,14},{18,16},{20... | collective-permute-start | bytes 208904 | tf_op jit(solution)/shard_map/ppermute | solution.py:216
  16.1 43.8 %collective-permute-start = (bf16[128,16]{1,0:T(8,128)(2,1)}, bf16[128,16]{1,0:T(8,128)(2,1)S(1)}, u32[]{:S(2)}, u32[]{:S(2)}) collective-permute-start(bf16[128,16]{1,0:T(8,128)(2,1)} %slice.158), channel_id=1, source_target_pairs={{0,2},{2,4},{4,6},{6,8},{8,10},{10,12},{12,14},{14,16},{16,18},{18... | collective-permute-start | bytes 12296 | tf_op jit(solution)/shard_map/ppermute | solution.py:215
  42.8 7.7 %copy-start.14 = (f32[32]{0:T(128)S(1)}, f32[32]{0:T(128)}, u32[]{:S(2)}) copy-start(f32[32]{0:T(128)} %param.16) | copy-start | bytes 388
  51.0 4.5 %copy-start.13 = (bf16[32]{0:T(256)(128)(2,1)}, bf16[32]{0:T(256)(128)(2,1)S(1)}, u32[]{:S(2)}) copy-start(bf16[32]{0:T(256)(128)(2,1)S(1)} %pad.64.clone) | copy-start | bytes 196
  52.3 3.2 copy-start.12
  52.3 3.9 %copy-start.6 = (f32[32,256]{1,0:T(8,128)S(1)}, f32[32,256]{1,0:T(8,128)}, u32[]{:S(2)}) copy-start(f32[32,256]{1,0:T(8,128)} %param.14) | copy-start | bytes 98308
  52.3 7.6 %copy-start.3 = (bf16[128,384]{1,0:T(8,128)(2,1)S(1)}, bf16[128,384]{1,0:T(8,128)(2,1)}, u32[]{:S(2)}) copy-start(bf16[128,384]{1,0:T(8,128)(2,1)} %param.12) | copy-start | bytes 294916
  58.1 5.7 %collective-permute-start.5 = (f32[128,208]{1,0:T(8,128)S(1)}, f32[128,208]{1,0:T(8,128)S(1)}, u32[]{:S(2)}, u32[]{:S(2)}) collective-permute-start(f32[128,208]{1,0:T(8,128)S(1)} %constant_dynamic-slice_fusion.2), channel_id=1, source_target_pairs={{0,1},{1,0},{2,3},{3,2},{4,5},{5,4},{6,7},{7,6},{8,9},{9,8},{10,11... | collective-permute-start | bytes 319496 | tf_op jit(solution)/shard_map/ppermute | solution.py:253
  61.1 8.6 %collective-permute-start.2 = (f32[480,64]{1,0:T(8,128)S(1)}, f32[480,64]{1,0:T(8,128)}, u32[]{:S(2)}, u32[]{:S(2)}) collective-permute-start(f32[480,64]{1,0:T(8,128)S(1)} %constant_dynamic-slice_fusion.3), channel_id=1, source_target_pairs={{0,1},{1,0},{2,3},{3,2},{4,5},{5,4},{6,7},{7,6},{8,9},{9,8},{10,11... | collective-permute-start | bytes 368648 | tf_op jit(solution)/shard_map/ppermute | solution.py:228
  131.1 1.6 copy-start.5
  133.2 2.9 copy-start.1
  135.0 134.2 %collective-permute-start.7 = (f32[640,64]{1,0:T(8,128)}, f32[640,64]{1,0:T(8,128)S(1)}, u32[]{:S(2)}, u32[]{:S(2)}) collective-permute-start(f32[640,64]{1,0:T(8,128)} %fusion.7), channel_id=1, source_target_pairs={{0,1},{1,0},{2,3},{3,2},{4,5},{5,4},{6,7},{7,6},{8,9},{9,8},{10,11... | collective-permute-start | bytes 491528 | tf_op jit(solution)/shard_map/ppermute | solution.py:319
  139.0 130.2 %copy-start.2 = (f32[192,32]{1,0:T(8,128)S(1)}, f32[192,32]{1,0:T(8,128)}, u32[]{:S(2)}) copy-start(f32[192,32]{1,0:T(8,128)} %copy-done.1) | copy-start | bytes 73732
  139.0 131.7 %copy-start.8 = (s32[384]{0:T(512)S(1)}, s32[384]{0:T(512)}, u32[]{:S(2)}) copy-start(s32[384]{0:T(512)} %copy-done.7) | copy-start | bytes 4612
  139.0 131.7 %copy-start.9 = (s32[384]{0:T(512)S(1)}, s32[384]{0:T(512)}, u32[]{:S(2)}) copy-start(s32[384]{0:T(512)} %param.18) | copy-start | bytes 4612
  139.1 131.7 %copy-start.11 = (s32[128]{0:T(128)S(1)}, s32[128]{0:T(128)}, u32[]{:S(2)}) copy-start(s32[128]{0:T(128)} %copy-done.10) | copy-start | bytes 1540
  139.9 131.9 %copy-start.4 = (bf16[128,384]{1,0:T(8,128)(2,1)S(1)}, bf16[128,384]{1,0:T(8,128)(2,1)}, u32[]{:S(2)}) copy-start(bf16[128,384]{1,0:T(8,128)(2,1)} %param.12) | copy-start | bytes 294916
  140.1 128.3 %collective-permute-start.6 = (f32[128,192]{1,0:T(8,128)S(1)}, f32[128,192]{1,0:T(8,128)S(1)}, u32[]{:S(2)}, u32[]{:S(2)}) collective-permute-start(f32[128,192]{1,0:T(8,128)S(1)} %get-tuple-element.24), channel_id=1, source_target_pairs={{0,1},{1,0},{2,3},{3,2},{4,5},{5,4},{6,7},{7,6},{8,9},{9,8},{10,11... | collective-permute-start | bytes 294920 | tf_op jit(solution)/shard_map/ppermute | solution.py:338
  269.5 2.3 collective-permute-start.8
Sparse Core Ops, SparseCore 0:
  140.1 126.5 all-reduce.11

commit v2 on v1

--- a/solution.py
+++ b/solution.py
@@ -21,8 +21,8 @@
 
 
 def kernel(
-    plan, info, left, right, bias, mats, expand, head, cots, pred, grad_left, grad_right, wgrad,
-    x0, h0, s0, x1, h1, s1, g2, hg2, b1, wacc,
+    plan, info, left, right, bias, weights, expand, head, cots, pred, grad_left, grad_right,
+    wgrad, x0, h0, s0, x1, h1, s1, g2, hg2, b1, wacc, mats,
 ):
     sub, groups, total, n1, n2, n3, n4 = plan
     lanes = 256
@@ -66,6 +66,37 @@
             mats[mat],
             preferred_element_type=jnp.float32,
         )
+
+    width = 2 * lanes
+
+    def diag_of(slot):
+        return jnp.where(slot < 8, slot, jnp.where(slot < 12, slot - 12, slot - 4))
+
+    delta = diag_of(
+        lax.shift_right_logical(lax.broadcasted_iota(jnp.int32, (width, lanes), 0), 5)
+    ) - lax.shift_right_logical(lax.broadcasted_iota(jnp.int32, (width, lanes), 1), 5)
+    repeat = (
+        lax.broadcasted_iota(jnp.int32, (32, lanes), 0)
+        == lax.broadcasted_iota(jnp.int32, (32, lanes), 1) & 31
+    ).astype(jnp.bfloat16)
+    for mat, layer, sign, step in (
+        (0, 0, 1, dil_one), (1, 1, 1, dil_two), (2, 1, -1, dil_two), (3, 0, -1, dil_one)
+    ):
+        for along in range(3):
+            taken = along if sign > 0 else 2 - along
+            total_mat = jnp.zeros((width, lanes), jnp.float32)
+            for b in range(3):
+                spread = lax.dot_general(
+                    weights[layer, 3 * taken + b], repeat,
+                    (((0 if sign > 0 else 1,), (0,)), ((), ())),
+                    preferred_element_type=jnp.float32,
+                )
+                total_mat = jnp.where(
+                    delta == sign * (b - 1) * step,
+                    jnp.concatenate([spread] * 16, axis=0),
+                    total_mat,
+                )
+            mats[mat, along * width : (along + 1) * width] = total_mat.astype(jnp.bfloat16)
 
     n0 = 4
 
@@ -102,9 +133,12 @@
     def _(block):
         start = 2 * MAXDIL + block * n2
         t = jnp.tanh(conv(x1, h1, 1, start, n2, dil_two))
+        t_high = t.astype(jnp.bfloat16)
+        t_low = (t - t_high.astype(jnp.float32)).astype(jnp.bfloat16)
         scored = lax.dot_general(
-            head[...], t.astype(jnp.bfloat16), (((1,), (1,)), ((), ())),
-            preferred_element_type=jnp.float32,
+            head[...], t_high, (((1,), (1,)), ((), ())), preferred_element_type=jnp.float32
+        ) + lax.dot_general(
+            head[...], t_low, (((1,), (1,)), ((), ())), preferred_element_type=jnp.float32
         )
         pred[block] = scored[:PACK] + scored[PACK:]
         factor = lax.dot_general(
@@ -126,12 +160,12 @@
                 preferred_element_type=jnp.float32,
             )
 
-        width = 2 * lanes
         out_diag = lax.shift_right_logical(
             lax.broadcasted_iota(jnp.int32, (lanes, width), 0), 5
         )
-        slot = lax.shift_right_logical(lax.broadcasted_iota(jnp.int32, (lanes, width), 1), 5)
-        in_diag = jnp.where(slot < 8, slot, jnp.where(slot < 12, slot - 12, slot - 4))
+        in_diag = diag_of(
+            lax.shift_right_logical(lax.broadcasted_iota(jnp.int32, (lanes, width), 1), 5)
+        )
         fold = (
             lax.broadcasted_iota(jnp.int32, (width, 32), 0) & 31
             == lax.broadcasted_iota(jnp.int32, (width, 32), 1)
@@ -174,18 +208,74 @@
                 grad_right[half, at, :] = grad_right[half, at, :] + piece
 
 
-def tap_matrix(weight, dilation, sign):
-    diags = jnp.array([0, 1, 2, 3, 4, 5, 6, 7, -4, -3, -2, -1, 8, 9, 10, 11], jnp.int32)
-    outs, ins = weight.shape[1], weight.shape[2]
-    weight = weight.reshape(3, 3, outs, ins)
-    if sign < 0:
-        weight = weight[::-1]
-    total = jnp.zeros((3, 16, ins, PACK, outs), weight.dtype)
-    for b in range(3):
-        hit = diags[:, None] == jnp.arange(PACK)[None, :] + sign * (b - 1) * dilation
-        spread = jnp.transpose(weight[:, b], (0, 2, 1))[:, None, :, None, :]
-        total = jnp.where(hit[None, :, None, :, None], spread, total)
-    return total.reshape(3 * 16 * ins, PACK * outs)
+def swapped(me, bit):
+    return me + bit - 2 * bit * ((me // bit) % 2)
+
+
+def tail(
+    plan, both_in, conv_in, embeddings, projection, embed_out, proj_out, conv_out,
+    both, both_slots, conv, conv_slots, spill_slot, sums, sum_slots, send, recv,
+):
+    n_bin, n_diag, rows, scaling = plan
+    me_bin, me_diag = lax.axis_index("bin"), lax.axis_index("diag")
+    diag_bits = [1 << k for k in range(n_diag.bit_length() - 1)]
+    bin_bits = [1 << k for k in range(n_bin.bit_length() - 1)]
+    after = {"bin": (me_bin + 1) % n_bin}
+    before = {"bin": (me_bin + n_bin - 1) % n_bin}
+    partners = [{"diag": swapped(me_diag, bit)} for bit in diag_bits]
+    partners += [{"bin": swapped(me_bin, bit)} for bit in bin_bits]
+    barrier = pltpu.get_barrier_semaphore()
+    for partner in partners + [after, before]:
+        pl.semaphore_signal(
+            barrier, inc=1, device_id=partner, device_id_type=pl.DeviceIdType.MESH
+        )
+    pl.semaphore_wait(barrier, len(partners) + 2)
+
+    def copy(source, target, at, device):
+        return pltpu.make_async_remote_copy(
+            src_ref=source, dst_ref=target, send_sem=send.at[at], recv_sem=recv.at[at],
+            device_id=device, device_id_type=pl.DeviceIdType.MESH,
+        )
+
+    both[...] = both_in[...]
+    conv[...] = conv_in[...]
+    for k in range(len(diag_bits)):
+        first = copy(both, both_slots.at[k], 2 * k, partners[k])
+        second = copy(conv, conv_slots.at[k], 2 * k + 1, partners[k])
+        first.start()
+        second.start()
+        first.wait()
+        both[...] += both_slots[k]
+        second.wait()
+        conv[...] += conv_slots[k]
+    at = 2 * len(diag_bits)
+    half = both.shape[0] // 2
+    spill = both.shape[1] - rows
+    hop = copy(both.at[pl.ds(half, half), pl.ds(rows, spill)], spill_slot, at, after)
+    hop.start()
+    hop.wait()
+    both[half:, :spill] += spill_slot[...]
+    summed = both[:, :rows]
+    part = lax.dot_general(
+        summed, embeddings[...].astype(jnp.float32), (((1,), (1,)), ((), ())),
+        precision=HIGHEST, preferred_element_type=jnp.float32,
+    )
+    count = conv.shape[0]
+    sums[:count] = conv[...]
+    sums[count:] = jnp.zeros_like(sums[count:])
+    sums[count:, : part.shape[1]] = part
+    for k in range(len(bin_bits)):
+        step = copy(sums, sum_slots.at[k], at + 1 + k, partners[len(diag_bits) + k])
+        step.start()
+        if k == 0:
+            embed_out[...] = lax.dot_general(
+                projection[...].astype(jnp.float32), summed, (((1,), (0,)), ((), ())),
+                precision=HIGHEST, preferred_element_type=jnp.float32,
+            )
+        step.wait()
+        sums[...] += sum_slots[k]
+    conv_out[...] = sums[:count] * scaling
+    proj_out[...] = sums[count:, : part.shape[1]] * scaling
 
 
 def split_two(x):
@@ -268,14 +358,6 @@
     cots = jnp.concatenate([cot_high, cot_low, cot_high, jnp.zeros_like(cot_high)], axis=1)
     expand = jnp.concatenate([spread(head_high), spread(head_high), spread(head_low), pad])
     head = jnp.concatenate([spread(head_high), spread(head_low)])
-    mats = jnp.stack(
-        [
-            tap_matrix(conv_weight[0], dilations[0], 1),
-            tap_matrix(conv_weight[1], dilations[1], 1),
-            tap_matrix(jnp.transpose(conv_weight[1], (0, 2, 1)), dilations[1], -1),
-            tap_matrix(jnp.transpose(conv_weight[0], (0, 2, 1)), dilations[0], -1),
-        ]
-    )
     info = jnp.concatenate([dilations, (first_row + me * sub - HALO)[None].astype(jnp.int32)])
 
     writes = sub + PACK * (groups - 1)
@@ -295,12 +377,11 @@
         + [
             pltpu.VMEM((region, groups, lanes), jnp.float32),
             pltpu.VMEM((lanes, 6 * lanes), jnp.float32),
+            pltpu.VMEM((4, 6 * lanes, lanes), jnp.bfloat16),
         ],
         compiler_params=pltpu.CompilerParams(vmem_limit_bytes=60 * 1024 * 1024),
         name="band",
-    )(info, halves(left), halves(right), bias, mats, expand, head, cots)
-
-    conv_sum = lax.psum(conv_part, ("bin", "diag"))
+    )(info, halves(left), halves(right), bias, conv_weight, expand, head, cots)
 
     grad_right = jnp.concatenate([grad_right[0], grad_right[1]], axis=1)
     spilled = jnp.zeros((sub + diags, channels), jnp.float32)
@@ -314,18 +395,37 @@
     buffer = lax.dynamic_update_slice_in_dim(
         jnp.zeros((rows_dev + diags, 2 * channels), jnp.float32), own, me * sub, 0
     )
-    both = buffer
-    for k in range(1, n_diag):
-        both = both + lax.ppermute(buffer, "diag", pairs(k))
-    incoming = lax.ppermute(both[rows_dev:, channels:], "bin", shifted("bin", n_bin, 1))
-    both = both[:rows_dev] + jnp.pad(incoming, ((0, rows_dev - diags), (channels, 0)))
-    grad_embed = jnp.einsum(
-        "ek,bk->eb", projection.astype(jnp.float32), both, precision=HIGHEST
-    )
-    proj_part = jnp.einsum(
-        "eb,bk->ek", embeddings.astype(jnp.float32), both, precision=HIGHEST
-    )
-    proj_sum = lax.psum(proj_part, "bin")
+    conv_rows = conv_part.size // 128
+    features = embeddings.shape[0]
+    scaling = 1.0 / math.sqrt(total_bins * diags)
+    wide_both = (2 * channels, rows_dev + diags)
+    diag_steps, bin_steps = n_diag.bit_length() - 1, n_bin.bit_length() - 1
+    sum_rows = conv_rows + 2 * channels
+    grad_embed, proj_sum, conv_sum = pl.pallas_call(
+        functools.partial(tail, (n_bin, n_diag, rows_dev, scaling)),
+        out_shape=[
+            jax.ShapeDtypeStruct((features, rows_dev), jnp.float32),
+            jax.ShapeDtypeStruct((2 * channels, features), jnp.float32),
+            jax.ShapeDtypeStruct((conv_rows, 128), jnp.float32),
+        ],
+        in_specs=[vmem] * 4,
+        out_specs=[vmem] * 3,
+        scratch_shapes=[
+            pltpu.VMEM(wide_both, jnp.float32),
+            pltpu.VMEM((diag_steps,) + wide_both, jnp.float32),
+            pltpu.VMEM((conv_rows, 128), jnp.float32),
+            pltpu.VMEM((diag_steps, conv_rows, 128), jnp.float32),
+            pltpu.VMEM((channels, diags), jnp.float32),
+            pltpu.VMEM((sum_rows, 128), jnp.float32),
+            pltpu.VMEM((bin_steps, sum_rows, 128), jnp.float32),
+            pltpu.SemaphoreType.DMA((2 * diag_steps + 1 + bin_steps,)),
+            pltpu.SemaphoreType.DMA((2 * diag_steps + 1 + bin_steps,)),
+        ],
+        compiler_params=pltpu.CompilerParams(collective_id=0, has_side_effects=True),
+        name="tail",
+    )(jnp.transpose(buffer), conv_part.reshape(conv_rows, 128), embeddings, projection)
+    grad_proj = jnp.transpose(proj_sum)
+    grad_conv = conv_sum.reshape(conv_part.shape)
 
     pred = jnp.transpose(pred.reshape(blocks, PACK, n2, groups), (3, 1, 0, 2)).reshape(
         diags, cot_span
@@ -340,8 +440,7 @@
             pred_local, piece, lax.rem(me - k + n_diag, n_diag) * sub, 1
         )
     pred_local = jnp.where(counted, pred_local, 0.0)
-    scaling = 1.0 / math.sqrt(total_bins * diags)
-    return (pred_local, grad_embed, scaling * proj_sum, scaling * conv_sum)
+    return (pred_local, grad_embed, grad_proj, grad_conv)
 
 
 def solution(mesh):

time: 345 us -> 143 us (0.41)
  waiting for transfers between devices: 129 us -> 5.42 us
  blocking collectives: 63.2 us -> 0 us
  Pallas kernels: 57.6 us -> 90.2 us
  between operations: 15.9 us -> 1.06 us
  local copies, waits for them, and re-layouts: 35.9 us -> 21.1 us
  other arithmetic: 24.1 us -> 9.65 us
    psum x1 -> x0, waiting for transfers between devices: 125 us -> none  [on_device(): conv_sum = lax.psum(conv_part, ('bin', 'diag'))]
    psum x1 -> x0, blocking collectives: 63.2 us -> none  [on_device(): proj_sum = lax.psum(proj_part, 'bin')]
    pallas_call x0 -> x1, Pallas kernels: none -> 29.8 us  [on_device(): pl.pallas_call(functools.partial(tail, (n_bin, n_diag, rows_dev, scaling)...]
    select_n x4 -> x0, local copies, waits for them, and re-layouts: 17.3 us -> none  [tap_matrix(): total = jnp.where(hit[None, :, None, :, None], spread, total)]
    select_n x1 -> x0, other arithmetic: 5.78 us -> none  [tap_matrix(): total = jnp.where(hit[None, :, None, :, None], spread, total)]
    unnamed x34 -> x20, local copies, waits for them, and re-layouts: 1.16 us -> 6.44 us
  transfers between devices with their start and end apart: 10 -> 7, of which waited for: 4 -> 2; matrix products, arithmetic and copies ran while one was open for 15% -> 11% of each run, Pallas kernels for 0% -> 21%
where the time goes in v2:
time: 143 us; the launch traced here: 142 us
  Pallas kernels  90.2 us (63%)
  local copies, waits for them, and re-layouts  21.1 us (15%)
  starting transfers between devices  14.4 us (10%)
  other arithmetic  9.65 us (7%)
  waiting for transfers between devices  5.42 us (4%)
    pallas_call x1, Pallas kernels, on_device(): pl.pallas_call(functools.partial(kernel, (sub, groups, total_bins, n1, n2...  60.4 us
    pallas_call x1, Pallas kernels, on_device(): pl.pallas_call(functools.partial(tail, (n_bin, n_diag, rows_dev, scaling)...  29.8 us
    ppermute x2, starting transfers between devices, around(): lax.ppermute(block[:, rows_dev - before:], 'bin', shifted('bin', n_bin, 1))  8.11 us
    unnamed x20, local copies, waits for them, and re-layouts  6.44 us
    ppermute x2, starting transfers between devices, on_device(): piece = lax.ppermute(piece, 'diag', pairs(k))  3.08 us
    ppermute x2, waiting for transfers between devices, on_device(): piece = lax.ppermute(piece, 'diag', pairs(k))  3.01 us
  transfers between devices with their start and end apart: 7, of which 2 were waited for; matrix products, arithmetic and copies ran while one was open for 11% of the time, Pallas kernels for 21%

profile of v2, /device:TPU:0, one launch (start us, length us, event | category | flops | bytes accessed | tf_op | source)
XLA Modules:
  0.0 142.2 jit_solution(8382153190229535533)
XLA Ops:
  0.7 1.0 fusion.8
  1.8 2.4 %collective-permute-start.3 = (f32[128,8]{1,0:T(8,128)S(1)}, f32[128,8]{1,0:T(8,128)S(1)}, u32[]{:S(2)}, u32[]{:S(2)}) collective-permute-start(f32[128,8]{1,0:T(8,128)S(1)} %get-tuple-element.42), channel_id=1, source_target_pairs={{0,2},{2,4},{4,6},{6,8},{8,10},{10,12},{12,14},{14,16},{16,18},{18... | collective-permute-start | bytes 12296 | tf_op jit(solution)/shard_map/ppermute | solution.py:305
  4.2 1.3 collective-permute-start.4
  5.5 1.3 collective-permute-start.1
  6.8 0.8 slice.82
  7.6 5.8 %collective-permute-start = (bf16[128,16]{1,0:T(8,128)(2,1)S(1)}, bf16[128,16]{1,0:T(8,128)(2,1)S(1)}, u32[]{:S(2)}, u32[]{:S(2)}) collective-permute-start(bf16[128,16]{1,0:T(8,128)(2,1)S(1)} %slice.82), channel_id=1, source_target_pairs={{0,2},{2,4},{4,6},{6,8},{8,10},{10,12},{12,14},{14,16},{16,18},{18... | collective-permute-start | bytes 12296 | tf_op jit(solution)/shard_map/ppermute | solution.py:305
  13.4 0.7 fusion.16
  14.6 0.6 pad_maximum_fusion.3.head
  15.2 0.7 maximum_maximum_fusion.1.expand
  15.9 1.3 pad_add_fusion.1.info
  17.2 0.9 copy.35
  18.0 0.7 reshape.70.bias
  18.7 1.4 copy.41.projection
  20.2 0.2 pad_maximum_fusion.1
  20.4 1.6 %collective-permute-start.5 = (f32[128,208]{1,0:T(8,128)S(1)}, f32[128,208]{1,0:T(8,128)S(1)}, u32[]{:S(2)}, u32[]{:S(2)}) collective-permute-start(f32[128,208]{1,0:T(8,128)S(1)} %constant_dynamic-slice_fusion.2), channel_id=1, source_target_pairs={{0,1},{1,0},{2,3},{3,2},{4,5},{5,4},{6,7},{7,6},{8,9},{9,8},{10,11... | collective-permute-start | bytes 319496 | tf_op jit(solution)/shard_map/ppermute | solution.py:343
  22.2 0.3 fusion
  22.5 0.6 collective-permute-start.2
  23.1 3.0 %collective-permute-done.5 = f32[128,208]{1,0:T(8,128)S(1)} collective-permute-done((f32[128,208]{1,0:T(8,128)S(1)}, f32[128,208]{1,0:T(8,128)S(1)}, u32[]{:S(2)}, u32[]{:S(2)}) %collective-permute-start.5) | collective-permute-done | bytes 106528 | tf_op jit(solution)/shard_map/ppermute | solution.py:343
  26.1 0.6 reshape.71
  26.7 1.1 copy.36
  27.9 0.3 reshape.72
  28.3 0.9 maximum_maximum_fusion.cots
  29.2 2.4 %collective-permute-done.2 = f32[480,64]{1,0:T(8,128)} collective-permute-done((f32[480,64]{1,0:T(8,128)S(1)}, f32[480,64]{1,0:T(8,128)}, u32[]{:S(2)}, u32[]{:S(2)}) %collective-permute-start.2) | collective-permute-done | bytes 122912 | tf_op jit(solution)/shard_map/ppermute | solution.py:318
  31.6 1.0 dynamic-slice_add_fusion
  32.6 0.6 fusion.14
  33.5 0.5 maximum_bitcast_fusion
  33.9 0.8 pad_maximum_fusion.right
  34.8 0.7 pad_maximum_fusion.2.left
  35.5 60.4 %band.1 = (f32[13,8,512]{2,1,0:T(8,128)}, f32[8,24,256]{2,1,0:T(8,128)}, f32[2,440,128]{2,1,0:T(8,128)}, f32[2,9,32,32]{3,2,1,0:T(8,128)}) custom-call(s32[3]{0:T(128)} %pad_add_fusion.1.info, f32[2,224,128]{2,1,0:T(8,128)} %pad_maximum_fusion.2.left, f32[2,472,128]{2,1,0:T(8,128)} %pad_maximum_fusion.right, f32[32,256]{1,0:T(8,128)} %reshape.70.bias, ...), custom_call_target="tpu_custom_call" | custom-call | tf_op jit(solution)/shard_map/band/pallas_call | solution.py:366
  95.9 1.3 copy.39
  97.3 0.2 reshape.75
  97.5 0.2 reduce_sum.9
  97.8 0.3 copy-done.2
  98.1 0.8 reshape.76.conv_in
  98.9 0.2 reshape.73
  99.1 1.8 %copy.37 = f32[13,8,16,32]{2,0,1,3:T(8,128)S(1)} copy(f32[13,8,16,32]{3,2,1,0:T(8,128)S(1)} %reshape.73) | data formatting | bytes 425984 | tf_op jit(solution)/shard_map/reshape | solution.py:430
  100.9 0.8 reshape.74
  101.8 1.5 %collective-permute-start.6 = (f32[128,192]{1,0:T(8,128)S(1)}, f32[128,192]{1,0:T(8,128)S(1)}, u32[]{:S(2)}, u32[]{:S(2)}) collective-permute-start(f32[128,192]{1,0:T(8,128)S(1)} %get-tuple-element.30), channel_id=1, source_target_pairs={{0,1},{1,0},{2,3},{3,2},{4,5},{5,4},{6,7},{7,6},{8,9},{9,8},{10,11... | collective-permute-start | bytes 294920 | tf_op jit(solution)/shard_map/ppermute | solution.py:438
  103.3 0.2 pad_add_fusion
  103.6 0.8 dynamic_update_slice.20
  104.4 0.7 copy-done
  105.0 29.8 %tail.1 = (f32[128,384]{1,0:T(8,128)}, f32[64,128]{1,0:T(8,128)}, f32[144,128]{1,0:T(8,128)}) custom-call(f32[64,640]{1,0:T(8,128)} %bitcast.32, f32[144,128]{1,0:T(8,128)} %reshape.76.conv_in, bf16[128,384]{1,0:T(8,128)(2,1)} %embeddings.1, bf16[128,64]{1,0:T(8,128)(2,1)} %copy.41.projection), custom_call_target="tpu_custom_call" | custom-call | tf_op jit(solution)/shard_map/tail/pallas_call | solution.py:404
  134.9 1.7 %reshape.77 = f32[2,9,32,32]{3,2,1,0:T(8,128)} reshape(f32[144,128]{1,0:T(8,128)} %get-tuple-element.17) | data formatting | bytes 147456 | tf_op jit(solution)/shard_map/reshape | solution.py:428
  136.6 0.9 dynamic_update_slice.18
  137.5 0.9 dynamic_update_slice.19
  138.4 0.8 fusion.7
  139.2 1.6 %copy.52 = f32[128,384]{1,0:T(8,128)} copy(f32[128,384]{1,0:T(8,128)} %get-tuple-element.55) | data formatting | bytes 393216
  140.8 1.4 copy.53
  (51 shorter events, 1.5 us)
Async XLA Ops:
  0.6 21.5 %copy-start.1 = (bf16[128,384]{1,0:T(8,128)(2,1)S(1)}, bf16[128,384]{1,0:T(8,128)(2,1)}, u32[]{:S(2)}) copy-start(bf16[128,384]{1,0:T(8,128)(2,1)} %embeddings.1) | copy-start | bytes 294916
  0.6 21.5 %copy-start.5 = (bf16[128,64]{0,1:T(8,128)(2,1)S(1)}, bf16[128,64]{0,1:T(8,128)(2,1)}, u32[]{:S(2)}) copy-start(bf16[128,64]{0,1:T(8,128)(2,1)} %param.9) | copy-start | bytes 49156
  1.8 18.3 %collective-permute-start.3 = (f32[128,8]{1,0:T(8,128)S(1)}, f32[128,8]{1,0:T(8,128)S(1)}, u32[]{:S(2)}, u32[]{:S(2)}) collective-permute-start(f32[128,8]{1,0:T(8,128)S(1)} %get-tuple-element.42), channel_id=1, source_target_pairs={{0,2},{2,4},{4,6},{6,8},{8,10},{10,12},{12,14},{14,16},{16,18},{18... | collective-permute-start | bytes 12296 | tf_op jit(solution)/shard_map/ppermute | solution.py:305
  4.2 16.0 %collective-permute-start.4 = (f32[128,8]{1,0:T(8,128)S(1)}, f32[128,8]{1,0:T(8,128)S(1)}, u32[]{:S(2)}, u32[]{:S(2)}) collective-permute-start(f32[128,8]{1,0:T(8,128)S(1)} %get-tuple-element.43), channel_id=1, source_target_pairs={{2,0},{4,2},{6,4},{8,6},{10,8},{12,10},{14,12},{16,14},{18,16},{20... | collective-permute-start | bytes 12296 | tf_op jit(solution)/shard_map/ppermute | solution.py:306
  5.5 16.7 %collective-permute-start.1 = (bf16[128,272]{1,0:T(8,128)(2,1)}, bf16[128,272]{1,0:T(8,128)(2,1)S(1)}, u32[]{:S(2)}, u32[]{:S(2)}) collective-permute-start(bf16[128,272]{1,0:T(8,128)(2,1)} %bitcast.33), channel_id=1, source_target_pairs={{2,0},{4,2},{6,4},{8,6},{10,8},{12,10},{14,12},{16,14},{18,16},{20... | collective-permute-start | bytes 208904 | tf_op jit(solution)/shard_map/ppermute | solution.py:306
  7.6 14.5 %collective-permute-start = (bf16[128,16]{1,0:T(8,128)(2,1)S(1)}, bf16[128,16]{1,0:T(8,128)(2,1)S(1)}, u32[]{:S(2)}, u32[]{:S(2)}) collective-permute-start(bf16[128,16]{1,0:T(8,128)(2,1)S(1)} %slice.82), channel_id=1, source_target_pairs={{0,2},{2,4},{4,6},{6,8},{8,10},{10,12},{12,14},{14,16},{16,18},{18... | collective-permute-start | bytes 12296 | tf_op jit(solution)/shard_map/ppermute | solution.py:305
  20.4 5.7 %collective-permute-start.5 = (f32[128,208]{1,0:T(8,128)S(1)}, f32[128,208]{1,0:T(8,128)S(1)}, u32[]{:S(2)}, u32[]{:S(2)}) collective-permute-start(f32[128,208]{1,0:T(8,128)S(1)} %constant_dynamic-slice_fusion.2), channel_id=1, source_target_pairs={{0,1},{1,0},{2,3},{3,2},{4,5},{5,4},{6,7},{7,6},{8,9},{9,8},{10,11... | collective-permute-start | bytes 319496 | tf_op jit(solution)/shard_map/ppermute | solution.py:343
  22.5 9.0 %collective-permute-start.2 = (f32[480,64]{1,0:T(8,128)S(1)}, f32[480,64]{1,0:T(8,128)}, u32[]{:S(2)}, u32[]{:S(2)}) collective-permute-start(f32[480,64]{1,0:T(8,128)S(1)} %constant_dynamic-slice_fusion.3), channel_id=1, source_target_pairs={{0,1},{1,0},{2,3},{3,2},{4,5},{5,4},{6,7},{7,6},{8,9},{9,8},{10,11... | collective-permute-start | bytes 368648 | tf_op jit(solution)/shard_map/ppermute | solution.py:318
  95.9 1.4 copy-start.4
  97.1 1.0 copy-start.2
  97.2 1.7 %copy-start.3 = (f32[13,8,512]{2,1,0:T(8,128)S(1)}, f32[13,8,512]{2,1,0:T(8,128)}, u32[]{:S(2)}) copy-start(f32[13,8,512]{2,1,0:T(8,128)} %get-tuple-element.11) | copy-start | bytes 638980
  101.7 36.7 %copy-start.6 = (s32[384]{0:T(512)S(1)}, s32[384]{0:T(512)}, u32[]{:S(2)}) copy-start(s32[384]{0:T(512)} %param.14) | copy-start | bytes 4612
  101.8 35.7 %collective-permute-start.6 = (f32[128,192]{1,0:T(8,128)S(1)}, f32[128,192]{1,0:T(8,128)S(1)}, u32[]{:S(2)}, u32[]{:S(2)}) collective-permute-start(f32[128,192]{1,0:T(8,128)S(1)} %get-tuple-element.30), channel_id=1, source_target_pairs={{0,1},{1,0},{2,3},{3,2},{4,5},{5,4},{6,7},{7,6},{8,9},{9,8},{10,11... | collective-permute-start | bytes 294920 | tf_op jit(solution)/shard_map/ppermute | solution.py:438
  104.4 0.7 copy-start

commit v3 on v2

--- a/solution.py
+++ b/solution.py
@@ -18,6 +18,18 @@
 
 def cut(rows, most):
     return max(n for n in range(1, most + 1) if rows % n == 0)
+
+
+def steps(blocks):
+    many = 2 if blocks % 2 == 0 else 3 if blocks % 3 == 0 else 1
+
+    def run(body):
+        @pl.loop(0, blocks // many)
+        def _(turn):
+            for u in range(many):
+                body(turn * many + u)
+
+    return run
 
 
 def kernel(
@@ -100,7 +112,7 @@
 
     n0 = 4
 
-    @pl.loop(0, (sub + 2 * HALO) // n0)
+    @steps((sub + 2 * HALO) // n0)
     def _(block):
         start = block * n0
         rows = []
@@ -114,22 +126,22 @@
         t = jnp.tanh(jnp.concatenate(rows, axis=0))
         keep = inside_rows(start, n0)
         s0[pl.ds(start, n0)] = (
-            jnp.where(keep, 1.0 - t * t, 0.0).astype(jnp.bfloat16).reshape(n0, groups, lanes)
+            jnp.where(keep, 1.0 - t * t, 0.0).reshape(n0, groups, lanes)
         )
         store(x0, h0, start, n0, jnp.where(keep, t, 0.0))
 
-    @pl.loop(0, (sub + 6 * MAXDIL) // n1)
+    @steps((sub + 6 * MAXDIL) // n1)
     def _(block):
         start = MAXDIL + block * n1
         t = jnp.tanh(conv(x0, h0, 0, start, n1, dil_one))
         keep = inside_rows(start, n1)
         s1[pl.ds(start, n1)] = (
-            jnp.where(keep, 1.0 - t * t, 0.0).astype(jnp.bfloat16).reshape(n1, groups, lanes)
+            jnp.where(keep, 1.0 - t * t, 0.0).reshape(n1, groups, lanes)
         )
         before = x0[pl.ds(start, n1)].reshape(n1 * groups, lanes).astype(jnp.float32)
         store(x1, h1, start, n1, jnp.where(keep, before + t, 0.0))
 
-    @pl.loop(0, (sub + 4 * MAXDIL) // n2)
+    @steps((sub + 4 * MAXDIL) // n2)
     def _(block):
         start = 2 * MAXDIL + block * n2
         t = jnp.tanh(conv(x1, h1, 1, start, n2, dil_two))
@@ -150,7 +162,7 @@
     def weight_grad(layer, g_ref, x_ref, h_ref, step):
         wacc[...] = jnp.zeros_like(wacc)
 
-        @pl.loop(0, sub // n4)
+        @steps(sub // n4)
         def _(block):
             start = HALO + block * n4
             wacc[...] += lax.dot_general(
@@ -183,22 +195,22 @@
 
     weight_grad(1, g2, x1, h1, dil_two)
 
-    @pl.loop(0, (sub + 2 * MAXDIL) // n3)
+    @steps((sub + 2 * MAXDIL) // n3)
     def _(block):
         start = 3 * MAXDIL + block * n3
         back = conv(g2, hg2, 2, start, n3, dil_two)
         b1[pl.ds(start, n3)] = back.reshape(n3, groups, lanes)
-        scale = s1[pl.ds(start, n3)].reshape(n3 * groups, lanes).astype(jnp.float32)
+        scale = s1[pl.ds(start, n3)].reshape(n3 * groups, lanes)
         store(x1, h1, start, n3, back * scale)
 
     weight_grad(0, x1, x0, h0, dil_one)
     grad_right[...] = jnp.zeros_like(grad_right)
 
-    @pl.loop(0, sub // n4)
+    @steps(sub // n4)
     def _(block):
         start = HALO + block * n4
         back = conv(x1, h1, 3, start, n4, dil_one)
-        scale = s0[pl.ds(start, n4)].reshape(n4 * groups, lanes).astype(jnp.float32)
+        scale = s0[pl.ds(start, n4)].reshape(n4 * groups, lanes)
         grad = (back + b1[pl.ds(start, n4)].reshape(n4 * groups, lanes)) * scale
         grad_left[block] = jnp.sum(grad.reshape(n4, groups, lanes), axis=1)
         for u in range(n4):
@@ -214,7 +226,8 @@
 
 def tail(
     plan, both_in, conv_in, embeddings, projection, embed_out, proj_out, conv_out,
-    both, both_slots, conv, conv_slots, spill_slot, sums, sum_slots, send, recv,
+    both, both_slots, conv_slots, spill_slot, sums, cut_slot, held, sum_slots, far_slot,
+    send, recv,
 ):
     n_bin, n_diag, rows, scaling = plan
     me_bin, me_diag = lax.axis_index("bin"), lax.axis_index("diag")
@@ -231,6 +244,10 @@
         )
     pl.semaphore_wait(barrier, len(partners) + 2)
 
+    near = partners[len(diag_bits)]
+    ids = iter(range(64))
+    count, half = conv_in.shape[0], both.shape[0] // 2
+
     def copy(source, target, at, device):
         return pltpu.make_async_remote_copy(
             src_ref=source, dst_ref=target, send_sem=send.at[at], recv_sem=recv.at[at],
@@ -238,21 +255,32 @@
         )
 
     both[...] = both_in[...]
-    conv[...] = conv_in[...]
+    sums[:count] = conv_in[...]
+    mine, theirs = me_bin % 2, 1 - me_bin % 2
+    conv_half, proj_half = count // 2, half
+
+    def exchange(rows_at, size, slot, device):
+        return copy(sums.at[pl.ds(rows_at, size)], slot, next(ids), device)
+
+    conv_cut = exchange(theirs * conv_half, conv_half, cut_slot.at[pl.ds(0, conv_half)], near)
+    conv_cut.start()
     for k in range(len(diag_bits)):
-        first = copy(both, both_slots.at[k], 2 * k, partners[k])
-        second = copy(conv, conv_slots.at[k], 2 * k + 1, partners[k])
+        first = copy(both, both_slots.at[k], next(ids), partners[k])
         first.start()
-        second.start()
         first.wait()
         both[...] += both_slots[k]
+    conv_cut.wait()
+    held[:conv_half] = sums[pl.ds(mine * conv_half, conv_half)] + cut_slot[:conv_half]
+    spill = both.shape[1] - rows
+    hop = copy(both.at[pl.ds(half, half), pl.ds(rows, spill)], spill_slot, next(ids), after)
+    hop.start()
+    for k in range(len(diag_bits)):
+        second = copy(
+            held.at[pl.ds(0, conv_half)], conv_slots.at[k], next(ids), partners[k]
+        )
+        second.start()
         second.wait()
-        conv[...] += conv_slots[k]
-    at = 2 * len(diag_bits)
-    half = both.shape[0] // 2
-    spill = both.shape[1] - rows
-    hop = copy(both.at[pl.ds(half, half), pl.ds(rows, spill)], spill_slot, at, after)
-    hop.start()
+        held[:conv_half] += conv_slots[k]
     hop.wait()
     both[half:, :spill] += spill_slot[...]
     summed = both[:, :rows]
@@ -260,22 +288,34 @@
         summed, embeddings[...].astype(jnp.float32), (((1,), (1,)), ((), ())),
         precision=HIGHEST, preferred_element_type=jnp.float32,
     )
-    count = conv.shape[0]
-    sums[:count] = conv[...]
+    features = part.shape[1]
     sums[count:] = jnp.zeros_like(sums[count:])
-    sums[count:, : part.shape[1]] = part
-    for k in range(len(bin_bits)):
-        step = copy(sums, sum_slots.at[k], at + 1 + k, partners[len(diag_bits) + k])
+    sums[count:, :features] = part
+    proj_cut = exchange(
+        count + theirs * proj_half, proj_half, cut_slot.at[pl.ds(conv_half, proj_half)], near
+    )
+    proj_cut.start()
+    embed_out[...] = lax.dot_general(
+        projection[...].astype(jnp.float32), summed, (((1,), (0,)), ((), ())),
+        precision=HIGHEST, preferred_element_type=jnp.float32,
+    )
+    proj_cut.wait()
+    held[conv_half:] = (
+        sums[pl.ds(count + mine * proj_half, proj_half)] + cut_slot[conv_half:]
+    )
+    for k in range(1, len(bin_bits)):
+        step = copy(held, sum_slots.at[k - 1], next(ids), partners[len(diag_bits) + k])
         step.start()
-        if k == 0:
-            embed_out[...] = lax.dot_general(
-                projection[...].astype(jnp.float32), summed, (((1,), (0,)), ((), ())),
-                precision=HIGHEST, preferred_element_type=jnp.float32,
-            )
         step.wait()
-        sums[...] += sum_slots[k]
-    conv_out[...] = sums[:count] * scaling
-    proj_out[...] = sums[count:, : part.shape[1]] * scaling
+        held[...] += sum_slots[k - 1]
+    last = copy(held, far_slot, next(ids), near)
+    last.start()
+    last.wait()
+    own, far = held[...] * scaling, far_slot[...] * scaling
+    conv_out[pl.ds(mine * conv_half, conv_half)] = own[:conv_half]
+    conv_out[pl.ds(theirs * conv_half, conv_half)] = far[:conv_half]
+    proj_out[pl.ds(mine * proj_half, proj_half)] = own[conv_half:, :features]
+    proj_out[pl.ds(theirs * proj_half, proj_half)] = far[conv_half:, :features]
 
 
 def split_two(x):
@@ -342,10 +382,10 @@
         if k:
             piece = lax.ppermute(piece, "diag", pairs(k))
         cot = lax.dynamic_update_index_in_dim(cot, piece, lax.rem(me - k + n_diag, n_diag), 0)
-    n1 = cut(sub + 6 * MAXDIL, 24)
-    n2 = cut(cot_span, 16)
-    n3 = cut(sub + 2 * MAXDIL, 25)
-    n4 = cut(sub, 24)
+    n1 = cut(sub + 6 * MAXDIL, 12)
+    n2 = cut(cot_span, 8)
+    n3 = cut(sub + 2 * MAXDIL, 10)
+    n4 = cut(sub, 16)
     blocks = cot_span // n2
     cot = jnp.transpose(cot.reshape(groups, PACK, blocks, n2), (2, 1, 3, 0)).reshape(
         blocks, PACK, n2 * groups
@@ -362,6 +402,7 @@
 
     writes = sub + PACK * (groups - 1)
     vmem = pl.BlockSpec(memory_space=pltpu.VMEM)
+    full_map = pltpu.VMEM((region, groups, lanes), jnp.float32)
     half_map = pltpu.VMEM((region, groups, lanes), jnp.bfloat16)
     pred, grad_left, grad_right, conv_part = pl.pallas_call(
         functools.partial(kernel, (sub, groups, total_bins, n1, n2, n3, n4)),
@@ -373,9 +414,13 @@
         ],
         in_specs=[pl.BlockSpec(memory_space=pltpu.SMEM)] + [vmem] * 7,
         out_specs=[vmem] * 4,
-        scratch_shapes=[half_map] * 8
+        scratch_shapes=[half_map] * 2
+        + [full_map]
+        + [half_map] * 2
+        + [full_map]
+        + [half_map] * 2
         + [
-            pltpu.VMEM((region, groups, lanes), jnp.float32),
+            full_map,
             pltpu.VMEM((lanes, 6 * lanes), jnp.float32),
             pltpu.VMEM((4, 6 * lanes, lanes), jnp.bfloat16),
         ],
@@ -413,13 +458,15 @@
         scratch_shapes=[
             pltpu.VMEM(wide_both, jnp.float32),
             pltpu.VMEM((diag_steps,) + wide_both, jnp.float32),
-            pltpu.VMEM((conv_rows, 128), jnp.float32),
-            pltpu.VMEM((diag_steps, conv_rows, 128), jnp.float32),
+            pltpu.VMEM((diag_steps, conv_rows // 2, 128), jnp.float32),
             pltpu.VMEM((channels, diags), jnp.float32),
             pltpu.VMEM((sum_rows, 128), jnp.float32),
-            pltpu.VMEM((bin_steps, sum_rows, 128), jnp.float32),
-            pltpu.SemaphoreType.DMA((2 * diag_steps + 1 + bin_steps,)),
-            pltpu.SemaphoreType.DMA((2 * diag_steps + 1 + bin_steps,)),
+            pltpu.VMEM((sum_rows // 2, 128), jnp.float32),
+            pltpu.VMEM((sum_rows // 2, 128), jnp.float32),
+            pltpu.VMEM((bin_steps - 1, sum_rows // 2, 128), jnp.float32),
+            pltpu.VMEM((sum_rows // 2, 128), jnp.float32),
+            pltpu.SemaphoreType.DMA((2 * diag_steps + bin_steps + 3,)),
+            pltpu.SemaphoreType.DMA((2 * diag_steps + bin_steps + 3,)),
         ],
         compiler_params=pltpu.CompilerParams(collective_id=0, has_side_effects=True),
         name="tail",

time: 143 us -> 162 us (1.13)
  local copies, waits for them, and re-layouts: 21.1 us -> 39.6 us
  waiting for transfers between devices: 5.42 us -> 0.02 us
  Pallas kernels: 90.2 us -> 92.8 us
  other arithmetic: 9.65 us -> 11.7 us
    dynamic_update_slice x2, local copies, waits for them, and re-layouts: 0.12 us -> 8.36 us  [on_device(): lax.dynamic_update_index_in_dim(cot, piece, lax.rem(me - k + n_diag, n_di...]
    pallas_call x1, Pallas kernels: 60.4 us -> 65.6 us  [on_device(): pl.pallas_call(functools.partial(kernel, (sub, groups, total_bins, n1, n2...]
    ppermute x2, waiting for transfers between devices: 3.01 us -> 0.01 us  [on_device(): piece = lax.ppermute(piece, 'diag', pairs(k))]
    pallas_call x1, Pallas kernels: 29.8 us -> 27.2 us  [on_device(): pl.pallas_call(functools.partial(tail, (n_bin, n_diag, rows_dev, scaling)...]
    ppermute x1, waiting for transfers between devices: 2.4 us -> 0.01 us  [on_device(): lax.ppermute(lax.dynamic_slice_in_dim(part, other * sub, span, 0), 'diag'...]
    reshape x1, local copies, waits for them, and re-layouts: 0.61 us -> 2.9 us  [on_device(): cot.reshape(groups, PACK, blocks, n2)]
    unnamed x20 -> x16, local copies, waits for them, and re-layouts: 6.44 us -> 8.7 us
    reshape x1, local copies, waits for them, and re-layouts: 0.78 us -> 2.97 us  [on_device(): jnp.transpose(pred.reshape(blocks, PACK, n2, groups), (3, 1, 0, 2))]
  transfers between devices with their start and end apart: 7 -> 7, of which waited for: 2 -> 0; matrix products, arithmetic and copies ran while one was open for 11% -> 19% of each run, Pallas kernels for 21% -> 17%
where the time goes in v3:
time: 162 us; the launch traced here: 161 us
  Pallas kernels  92.8 us (57%)
  local copies, waits for them, and re-layouts  39.6 us (24%)
  starting transfers between devices  14.4 us (9%)
  other arithmetic  11.7 us (7%)
    pallas_call x1, Pallas kernels, on_device(): pl.pallas_call(functools.partial(kernel, (sub, groups, total_bins, n1, n2...  65.6 us
    pallas_call x1, Pallas kernels, on_device(): pl.pallas_call(functools.partial(tail, (n_bin, n_diag, rows_dev, scaling)...  27.2 us
    unnamed x16, local copies, waits for them, and re-layouts  8.7 us
    dynamic_update_slice x2, local copies, waits for them, and re-layouts, on_device(): lax.dynamic_update_index_in_dim(cot, piece, lax.rem(me - k + n_diag, n_di...  8.36 us
    ppermute x2, starting transfers between devices, around(): lax.ppermute(block[:, rows_dev - before:], 'bin', shifted('bin', n_bin, 1))  8.12 us
  transfers between devices with their start and end apart: 7, of which 0 were waited for; matrix products, arithmetic and copies ran while one was open for 19% of the time, Pallas kernels for 17%

profile of v3, /device:TPU:0, one launch (start us, length us, event | category | flops | bytes accessed | tf_op | source)
XLA Modules:
  0.0 160.6 jit_solution(5994834670247677669)
XLA Ops:
  0.7 1.1 copy.54
  1.7 0.9 fusion.8
  2.6 2.4 %collective-permute-start.3 = (f32[128,8]{0,1:T(8,128)S(1)}, f32[128,8]{0,1:T(8,128)S(1)}, u32[]{:S(2)}, u32[]{:S(2)}) collective-permute-start(f32[128,8]{0,1:T(8,128)S(1)} %get-tuple-element.52), channel_id=1, source_target_pairs={{0,2},{2,4},{4,6},{6,8},{8,10},{10,12},{12,14},{14,16},{16,18},{18... | collective-permute-start | bytes 12296 | tf_op jit(solution)/shard_map/ppermute | solution.py:345
  5.0 1.3 collective-permute-start.4
  6.3 1.3 collective-permute-start.1
  7.6 0.8 slice.82
  8.4 5.8 %collective-permute-start = (bf16[128,16]{1,0:T(8,128)(2,1)S(1)}, bf16[128,16]{1,0:T(8,128)(2,1)S(1)}, u32[]{:S(2)}, u32[]{:S(2)}) collective-permute-start(bf16[128,16]{1,0:T(8,128)(2,1)S(1)} %slice.82), channel_id=1, source_target_pairs={{0,2},{2,4},{4,6},{6,8},{8,10},{10,12},{12,14},{14,16},{16,18},{18... | collective-permute-start | bytes 12296 | tf_op jit(solution)/shard_map/ppermute | solution.py:345
  14.2 0.7 fusion.16
  15.4 0.6 pad_maximum_fusion.3.head
  16.0 0.7 maximum_maximum_fusion.1.expand
  16.6 1.3 pad_add_fusion.1.info
  17.9 0.9 copy.53
  18.8 0.7 reshape.70.bias
  19.5 1.4 copy.62.projection
  21.0 1.6 collective-permute-start.5
  22.6 0.7 broadcast_in_dim.44
  23.3 4.2 %dynamic_update_slice.16 = f32[2,128,208]{1,0,2:T(2,128)} dynamic-update-slice(f32[2,128,208]{1,0,2:T(2,128)} %broadcast_in_dim.44, f32[1,128,208]{1,0,2:T(1,128)S(1)} %bitcast.47, s32[]{:T(128)S(6)} %select_n.45, s32[]{:T(128)} %constant.50.clone.1, s32[]{:T(128)} %constant.50.clone.1) | dynamic-update-slice | bytes 212996 | tf_op jit(solution)/shard_map/jit(dynamic_update_index_in_dim)/dynamic_update_slice | solution.py:384
  27.5 1.2 fusion
  28.7 0.7 copy-done
  29.4 0.7 constant_dynamic-slice_fusion.3
  30.7 4.2 %dynamic_update_slice.17 = f32[2,128,208]{1,0,2:T(2,128)} dynamic-update-slice(f32[2,128,208]{1,0,2:T(2,128)} %dynamic_update_slice.16, f32[1,128,208]{1,0,2:T(1,128)S(1)} %bitcast.48, s32[]{:T(128)S(6)} %select_n.47, s32[]{:T(128)} %constant.50.clone.1, s32[]{:T(128)} %constant.50.clone.1) | dynamic-update-slice | bytes 212996 | tf_op jit(solution)/shard_map/jit(dynamic_update_index_in_dim)/dynamic_update_slice | solution.py:384
  34.8 2.9 %reshape.71 = f32[32,8,26,8]{1,0,3,2:T(8,128)S(1)} reshape(f32[2,128,208]{1,0,2:T(2,128)} %dynamic_update_slice.17) | data formatting | bytes 425984 | tf_op jit(solution)/shard_map/reshape | solution.py:390
  37.7 1.8 %copy.65 = f32[26,8,256]{2,1,0:T(8,128)} copy(f32[26,8,256]{1,2,0:T(8,128)S(1)} %bitcast.39) | data formatting | bytes 425984 | tf_op jit(solution)/shard_map/reshape | solution.py:390
  39.6 1.1 subtract_convert_fusion
  40.6 1.0 maximum_maximum_fusion.cots
  41.6 1.1 dynamic-slice_add_fusion
  44.1 0.8 pad_maximum_fusion.right
  44.9 0.7 pad_maximum_fusion.1.left
  45.6 65.6 %band.1 = (f32[26,8,256]{2,1,0:T(8,128)}, f32[12,16,256]{2,1,0:T(8,128)}, f32[2,440,128]{2,1,0:T(8,128)}, f32[2,9,32,32]{3,2,1,0:T(8,128)}) custom-call(s32[3]{0:T(128)} %pad_add_fusion.1.info, f32[2,224,128]{2,1,0:T(8,128)} %pad_maximum_fusion.1.left, f32[2,472,128]{2,1,0:T(8,128)} %pad_maximum_fusion.right, f32[32,256]{1,0:T(8,128)} %reshape.70.bias, ...), custom_call_target="tpu_custom_call" | custom-call | tf_op jit(solution)/shard_map/band/pallas_call | solution.py:407
  111.2 1.3 copy.60
  112.5 0.7 fusion.11
  113.2 0.7 fusion.12
  113.9 1.1 reshape.75
  115.3 0.7 copy.59
  116.0 0.8 reshape.76.conv_in
  116.7 1.9 %copy.66 = f32[26,8,256]{1,2,0:T(8,128)S(1)} copy(f32[26,8,256]{2,1,0:T(8,128)} %get-tuple-element.11) | data formatting | bytes 425984 | tf_op jit(solution)/shard_map/reshape | solution.py:477
  118.7 3.0 %reshape.74 = f32[256,208]{0,1:T(8,128)} reshape(f32[32,8,26,8]{1,0,3,2:T(8,128)S(1)} %bitcast.40) | data formatting | bytes 425984 | tf_op jit(solution)/shard_map/reshape | solution.py:477
  121.6 0.9 slice.121
  122.6 1.6 collective-permute-start.6
  124.2 1.2 pad_add_fusion
  125.4 0.8 select_maximum_fusion
  126.2 0.8 dynamic_update_slice.20
  127.0 0.7 copy-done.1
  127.7 27.2 %tail.1 = (f32[128,384]{1,0:T(8,128)}, f32[64,128]{1,0:T(8,128)}, f32[144,128]{1,0:T(8,128)}) custom-call(f32[64,640]{1,0:T(8,128)} %bitcast.42, f32[144,128]{1,0:T(8,128)} %reshape.76.conv_in, bf16[128,384]{1,0:T(8,128)(2,1)} %embeddings.1, bf16[128,64]{1,0:T(8,128)(2,1)} %copy.62.projection), custom_call_target="tpu_custom_call" | custom-call | tf_op jit(solution)/shard_map/tail/pallas_call | solution.py:449
  154.9 1.7 %reshape.77 = f32[2,9,32,32]{3,2,1,0:T(8,128)} reshape(f32[144,128]{1,0:T(8,128)} %get-tuple-element.17) | data formatting | bytes 147456 | tf_op jit(solution)/shard_map/reshape | solution.py:475
  156.8 0.8 copy.63
  157.6 1.6 %copy.76 = f32[128,384]{1,0:T(8,128)} copy(f32[128,384]{1,0:T(8,128)} %get-tuple-element.65) | data formatting | bytes 393216
  159.3 1.4 copy.77
  (44 shorter events, 2.9 us)
Async XLA Ops:
  2.6 18.3 %collective-permute-start.3 = (f32[128,8]{0,1:T(8,128)S(1)}, f32[128,8]{0,1:T(8,128)S(1)}, u32[]{:S(2)}, u32[]{:S(2)}) collective-permute-start(f32[128,8]{0,1:T(8,128)S(1)} %get-tuple-element.52), channel_id=1, source_target_pairs={{0,2},{2,4},{4,6},{6,8},{8,10},{10,12},{12,14},{14,16},{16,18},{18... | collective-permute-start | bytes 12296 | tf_op jit(solution)/shard_map/ppermute | solution.py:345
  5.0 16.0 %collective-permute-start.4 = (f32[128,8]{0,1:T(8,128)S(1)}, f32[128,8]{0,1:T(8,128)S(1)}, u32[]{:S(2)}, u32[]{:S(2)}) collective-permute-start(f32[128,8]{0,1:T(8,128)S(1)} %get-tuple-element.53), channel_id=1, source_target_pairs={{2,0},{4,2},{6,4},{8,6},{10,8},{12,10},{14,12},{16,14},{18,16},{20... | collective-permute-start | bytes 12296 | tf_op jit(solution)/shard_map/ppermute | solution.py:346
  6.3 21.2 %collective-permute-start.1 = (bf16[128,272]{1,0:T(8,128)(2,1)}, bf16[128,272]{1,0:T(8,128)(2,1)S(1)}, u32[]{:S(2)}, u32[]{:S(2)}) collective-permute-start(bf16[128,272]{1,0:T(8,128)(2,1)} %bitcast.43), channel_id=1, source_target_pairs={{2,0},{4,2},{6,4},{8,6},{10,8},{12,10},{14,12},{16,14},{18,16},{20... | collective-permute-start | bytes 208904 | tf_op jit(solution)/shard_map/ppermute | solution.py:346
  8.4 19.1 %collective-permute-start = (bf16[128,16]{1,0:T(8,128)(2,1)S(1)}, bf16[128,16]{1,0:T(8,128)(2,1)S(1)}, u32[]{:S(2)}, u32[]{:S(2)}) collective-permute-start(bf16[128,16]{1,0:T(8,128)(2,1)S(1)} %slice.82), channel_id=1, source_target_pairs={{0,2},{2,4},{4,6},{6,8},{8,10},{10,12},{12,14},{14,16},{16,18},{18... | collective-permute-start | bytes 12296 | tf_op jit(solution)/shard_map/ppermute | solution.py:345
  21.0 9.7 %collective-permute-start.5 = (f32[128,208]{0,1:T(8,128)S(1)}, f32[128,208]{0,1:T(8,128)S(1)}, u32[]{:S(2)}, u32[]{:S(2)}) collective-permute-start(f32[128,208]{0,1:T(8,128)S(1)} %get-tuple-element.48), channel_id=1, source_target_pairs={{0,1},{1,0},{2,3},{3,2},{4,5},{5,4},{6,7},{7,6},{8,9},{9,8},{10,11... | collective-permute-start | bytes 319496 | tf_op jit(solution)/shard_map/ppermute | solution.py:383
  28.7 0.7 copy-start
  30.1 11.5 %collective-permute-start.2 = (f32[480,64]{1,0:T(8,128)}, f32[480,64]{1,0:T(8,128)}, u32[]{:S(2)}, u32[]{:S(2)}) collective-permute-start(f32[480,64]{1,0:T(8,128)} %constant_dynamic-slice_fusion.3), channel_id=1, source_target_pairs={{0,1},{1,0},{2,3},{3,2},{4,5},{5,4},{6,7},{7,6},{8,9},{9,8},{10,11... | collective-permute-start | bytes 368648 | tf_op jit(solution)/shard_map/ppermute | solution.py:358
  111.2 4.8 %copy-start.2 = (f32[2,9,32,32]{3,2,1,0:T(8,128)S(1)}, f32[2,9,32,32]{3,2,1,0:T(8,128)}, u32[]{:S(2)}) copy-start(f32[2,9,32,32]{3,2,1,0:T(8,128)} %get-tuple-element.14) | copy-start | bytes 221188
  118.7 38.0 %copy-start.3 = (s32[384]{0:T(512)S(1)}, s32[384]{0:T(512)}, u32[]{:S(2)}) copy-start(s32[384]{0:T(512)} %param.14) | copy-start | bytes 4612
  122.6 34.0 %collective-permute-start.6 = (f32[128,192]{0,1:T(8,128)S(1)}, f32[128,192]{0,1:T(8,128)S(1)}, u32[]{:S(2)}, u32[]{:S(2)}) collective-permute-start(f32[128,192]{0,1:T(8,128)S(1)} %get-tuple-element.50), channel_id=1, source_target_pairs={{0,1},{1,0},{2,3},{3,2},{4,5},{5,4},{6,7},{7,6},{8,9},{9,8},{10,11... | collective-permute-start | bytes 294920 | tf_op jit(solution)/shard_map/ppermute | solution.py:485
  127.0 0.7 copy-start.1

commit v4 on v3

--- a/solution.py
+++ b/solution.py
@@ -18,18 +18,6 @@
 
 def cut(rows, most):
     return max(n for n in range(1, most + 1) if rows % n == 0)
-
-
-def steps(blocks):
-    many = 2 if blocks % 2 == 0 else 3 if blocks % 3 == 0 else 1
-
-    def run(body):
-        @pl.loop(0, blocks // many)
-        def _(turn):
-            for u in range(many):
-                body(turn * many + u)
-
-    return run
 
 
 def kernel(
@@ -112,7 +100,7 @@
 
     n0 = 4
 
-    @steps((sub + 2 * HALO) // n0)
+    @pl.loop(0, (sub + 2 * HALO) // n0)
     def _(block):
         start = block * n0
         rows = []
@@ -126,22 +114,22 @@
         t = jnp.tanh(jnp.concatenate(rows, axis=0))
         keep = inside_rows(start, n0)
         s0[pl.ds(start, n0)] = (
-            jnp.where(keep, 1.0 - t * t, 0.0).reshape(n0, groups, lanes)
+            jnp.where(keep, 1.0 - t * t, 0.0).astype(jnp.bfloat16).reshape(n0, groups, lanes)
         )
         store(x0, h0, start, n0, jnp.where(keep, t, 0.0))
 
-    @steps((sub + 6 * MAXDIL) // n1)
+    @pl.loop(0, (sub + 6 * MAXDIL) // n1)
     def _(block):
         start = MAXDIL + block * n1
         t = jnp.tanh(conv(x0, h0, 0, start, n1, dil_one))
         keep = inside_rows(start, n1)
         s1[pl.ds(start, n1)] = (
-            jnp.where(keep, 1.0 - t * t, 0.0).reshape(n1, groups, lanes)
+            jnp.where(keep, 1.0 - t * t, 0.0).astype(jnp.bfloat16).reshape(n1, groups, lanes)
         )
         before = x0[pl.ds(start, n1)].reshape(n1 * groups, lanes).astype(jnp.float32)
         store(x1, h1, start, n1, jnp.where(keep, before + t, 0.0))
 
-    @steps((sub + 4 * MAXDIL) // n2)
+    @pl.loop(0, (sub + 4 * MAXDIL) // n2)
     def _(block):
         start = 2 * MAXDIL + block * n2
         t = jnp.tanh(conv(x1, h1, 1, start, n2, dil_two))
@@ -162,7 +150,7 @@
     def weight_grad(layer, g_ref, x_ref, h_ref, step):
         wacc[...] = jnp.zeros_like(wacc)
 
-        @steps(sub // n4)
+        @pl.loop(0, sub // n4)
         def _(block):
             start = HALO + block * n4
             wacc[...] += lax.dot_general(
@@ -195,22 +183,22 @@
 
     weight_grad(1, g2, x1, h1, dil_two)
 
-    @steps((sub + 2 * MAXDIL) // n3)
+    @pl.loop(0, (sub + 2 * MAXDIL) // n3)
     def _(block):
         start = 3 * MAXDIL + block * n3
         back = conv(g2, hg2, 2, start, n3, dil_two)
         b1[pl.ds(start, n3)] = back.reshape(n3, groups, lanes)
-        scale = s1[pl.ds(start, n3)].reshape(n3 * groups, lanes)
+        scale = s1[pl.ds(start, n3)].reshape(n3 * groups, lanes).astype(jnp.float32)
         store(x1, h1, start, n3, back * scale)
 
     weight_grad(0, x1, x0, h0, dil_one)
     grad_right[...] = jnp.zeros_like(grad_right)
 
-    @steps(sub // n4)
+    @pl.loop(0, sub // n4)
     def _(block):
         start = HALO + block * n4
         back = conv(x1, h1, 3, start, n4, dil_one)
-        scale = s0[pl.ds(start, n4)].reshape(n4 * groups, lanes)
+        scale = s0[pl.ds(start, n4)].reshape(n4 * groups, lanes).astype(jnp.float32)
         grad = (back + b1[pl.ds(start, n4)].reshape(n4 * groups, lanes)) * scale
         grad_left[block] = jnp.sum(grad.reshape(n4, groups, lanes), axis=1)
         for u in range(n4):
@@ -218,6 +206,88 @@
             for half in range(2):
                 piece = grad[u * groups : (u + 1) * groups, 128 * half : 128 * (half + 1)]
                 grad_right[half, at, :] = grad_right[half, at, :] + piece
+
+
+def opening(
+    plan, embeddings, projection, cot_in, projected, cot_out,
+    low, high, cot_low, cot_high, parts, part_slots, cots, cot_slots, send, recv,
+):
+    n_bin, n_diag, sub, span, cot_span = plan
+    me_bin, me_diag = lax.axis_index("bin"), lax.axis_index("diag")
+    rows = embeddings.shape[1]
+    after = {"bin": (me_bin + 1) % n_bin}
+    before = {"bin": (me_bin + n_bin - 1) % n_bin}
+    others = [{"diag": (me_diag + k) % n_diag} for k in range(1, n_diag)]
+    barrier = pltpu.get_barrier_semaphore()
+    for partner in others + [after, before]:
+        pl.semaphore_signal(
+            barrier, inc=1, device_id=partner, device_id_type=pl.DeviceIdType.MESH
+        )
+    pl.semaphore_wait(barrier, len(others) + 2)
+    ids = iter(range(64))
+
+    def copy(source, target, device):
+        at = next(ids)
+        made = pltpu.make_async_remote_copy(
+            src_ref=source, dst_ref=target, send_sem=send.at[at], recv_sem=recv.at[at],
+            device_id=device, device_id_type=pl.DeviceIdType.MESH,
+        )
+        made.start()
+        return made
+
+    first = [
+        copy(embeddings, high, before),
+        copy(embeddings.at[:, pl.ds(rows - 128, 128)], low, after),
+    ]
+    second = [
+        copy(cot_in.at[:, pl.ds(0, 128)], cot_high, before),
+        copy(cot_in.at[:, pl.ds(rows - 128, 128)], cot_low, after),
+    ]
+    has_low = (me_bin > 0).astype(jnp.float32)
+    has_high = (me_bin < n_bin - 1).astype(jnp.float32)
+    for made in first:
+        made.wait()
+    wide = jnp.concatenate(
+        [
+            low[...] * has_low.astype(jnp.bfloat16),
+            embeddings[...],
+            high[...] * has_high.astype(jnp.bfloat16),
+        ],
+        axis=1,
+    )
+    part = lax.dot_general(
+        projection[...], wide, (((0,), (0,)), ((), ())), preferred_element_type=jnp.float32
+    )
+    for d in range(n_diag):
+        at = 128 - HALO + d * sub
+        parts[d, :, :span] = part[:, at : at + span]
+        parts[d, :, span:] = jnp.zeros_like(parts[d, :, span:])
+    moves = [
+        copy(parts.at[(me_diag + k) % n_diag], part_slots.at[k - 1], others[k - 1])
+        for k in range(1, n_diag)
+    ]
+    for made in second:
+        made.wait()
+    cot = jnp.concatenate(
+        [cot_low[...] * has_low, cot_in[...], cot_high[...] * has_high], axis=1
+    )
+    for d in range(n_diag):
+        at = 128 - 2 * MAXDIL + d * sub
+        cots[d, :, :cot_span] = cot[:, at : at + cot_span]
+        cots[d, :, cot_span:] = jnp.zeros_like(cots[d, :, cot_span:])
+    cot_moves = [
+        copy(cots.at[(me_diag + k) % n_diag], cot_slots.at[k - 1], others[k - 1])
+        for k in range(1, n_diag)
+    ]
+    total = parts[me_diag]
+    for k in range(1, n_diag):
+        moves[k - 1].wait()
+        total = total + part_slots[k - 1]
+    projected[...] = jnp.transpose(total)
+    cot_out[me_diag] = cots[me_diag]
+    for k in range(1, n_diag):
+        cot_moves[k - 1].wait()
+        cot_out[(me_diag + n_diag - k) % n_diag] = cot_slots[k - 1]
 
 
 def swapped(me, bit):
@@ -323,10 +393,6 @@
     return high, (x - high.astype(jnp.float32)).astype(jnp.bfloat16)
 
 
-def shifted(axis, size, by):
-    return [(i, i + by) for i in range(size) if 0 <= i + by < size]
-
-
 def on_device(
     embeddings, projection, dist_bias, conv_weight, head_weight, dilations, band_limit, cotangent
 ):
@@ -341,23 +407,42 @@
     lanes = PACK * channels
     reach = HALO + diags
 
-    def around(block, before, after):
-        low = lax.ppermute(block[:, rows_dev - before :], "bin", shifted("bin", n_bin, 1))
-        high = lax.ppermute(block[:, :after], "bin", shifted("bin", n_bin, -1))
-        return jnp.concatenate([low, block, high], axis=1)
-
     def pairs(k):
         return [(i, (i + k) % n_diag) for i in range(n_diag)]
 
-    wide = around(embeddings, HALO, reach)
-    part = jnp.einsum("eb,ek->bk", wide, projection, preferred_element_type=jnp.float32)
+    row_ids = first_row + jnp.arange(rows_dev, dtype=jnp.int32)[None, :]
+    diag_ids = me * diag_dev + jnp.arange(diag_dev, dtype=jnp.int32)[:, None]
+    counted = (row_ids + diag_ids < total_bins) & (diag_ids < band_limit[None, :])
+    margin = 2 * MAXDIL
     span = sub + HALO + reach
-    projected = lax.dynamic_slice_in_dim(part, me * sub, span, 0)
-    for k in range(1, n_diag):
-        other = lax.rem(me + k, n_diag)
-        projected = projected + lax.ppermute(
-            lax.dynamic_slice_in_dim(part, other * sub, span, 0), "diag", pairs(k)
-        )
+    cot_span = sub + 2 * margin
+    wide_span, wide_cot = -(-span // 128) * 128, -(-cot_span // 128) * 128
+    features = embeddings.shape[0]
+    vmem = pl.BlockSpec(memory_space=pltpu.VMEM)
+    projected, cot = pl.pallas_call(
+        functools.partial(opening, (n_bin, n_diag, sub, span, cot_span)),
+        out_shape=[
+            jax.ShapeDtypeStruct((wide_span, 2 * channels), jnp.float32),
+            jax.ShapeDtypeStruct((n_diag, diag_dev, wide_cot), jnp.float32),
+        ],
+        in_specs=[vmem] * 3,
+        out_specs=[vmem] * 2,
+        scratch_shapes=[
+            pltpu.VMEM((features, 128), jnp.bfloat16),
+            pltpu.VMEM((features, rows_dev), jnp.bfloat16),
+            pltpu.VMEM((diag_dev, 128), jnp.float32),
+            pltpu.VMEM((diag_dev, 128), jnp.float32),
+            pltpu.VMEM((n_diag, 2 * channels, wide_span), jnp.float32),
+            pltpu.VMEM((n_diag - 1, 2 * channels, wide_span), jnp.float32),
+            pltpu.VMEM((n_diag, diag_dev, wide_cot), jnp.float32),
+            pltpu.VMEM((n_diag - 1, diag_dev, wide_cot), jnp.float32),
+            pltpu.SemaphoreType.DMA((2 + 2 * n_diag,)),
+            pltpu.SemaphoreType.DMA((2 + 2 * n_diag,)),
+        ],
+        compiler_params=pltpu.CompilerParams(collective_id=1, has_side_effects=True),
+        name="opening",
+    )(embeddings, projection, jnp.where(counted, cotangent, 0.0))
+    cot = cot[:, :, :cot_span]
     region = sub + 2 * HALO
     reads = region + PACK * (groups - 1)
     left = jnp.tile(projected[:region, :channels], (1, PACK))
@@ -369,23 +454,10 @@
         groups, lanes
     )
 
-    row_ids = first_row + jnp.arange(rows_dev, dtype=jnp.int32)[None, :]
-    diag_ids = me * diag_dev + jnp.arange(diag_dev, dtype=jnp.int32)[:, None]
-    counted = (row_ids + diag_ids < total_bins) & (diag_ids < band_limit[None, :])
-    margin = 2 * MAXDIL
-    cot_wide = around(jnp.where(counted, cotangent, 0.0), margin, margin)
-    cot_span = sub + 2 * margin
-    cot = jnp.zeros((n_diag, diag_dev, cot_span), jnp.float32)
-    for k in range(n_diag):
-        other = lax.rem(me + k, n_diag)
-        piece = lax.dynamic_slice_in_dim(cot_wide, other * sub, cot_span, 1)
-        if k:
-            piece = lax.ppermute(piece, "diag", pairs(k))
-        cot = lax.dynamic_update_index_in_dim(cot, piece, lax.rem(me - k + n_diag, n_diag), 0)
-    n1 = cut(sub + 6 * MAXDIL, 12)
-    n2 = cut(cot_span, 8)
-    n3 = cut(sub + 2 * MAXDIL, 10)
-    n4 = cut(sub, 16)
+    n1 = cut(sub + 6 * MAXDIL, 36)
+    n2 = cut(cot_span, 16)
+    n3 = cut(sub + 2 * MAXDIL, 40)
+    n4 = cut(sub, 32)
     blocks = cot_span // n2
     cot = jnp.transpose(cot.reshape(groups, PACK, blocks, n2), (2, 1, 3, 0)).reshape(
         blocks, PACK, n2 * groups
@@ -401,7 +473,6 @@
     info = jnp.concatenate([dilations, (first_row + me * sub - HALO)[None].astype(jnp.int32)])
 
     writes = sub + PACK * (groups - 1)
-    vmem = pl.BlockSpec(memory_space=pltpu.VMEM)
     full_map = pltpu.VMEM((region, groups, lanes), jnp.float32)
     half_map = pltpu.VMEM((region, groups, lanes), jnp.bfloat16)
     pred, grad_left, grad_right, conv_part = pl.pallas_call(
@@ -414,11 +485,7 @@
         ],
         in_specs=[pl.BlockSpec(memory_space=pltpu.SMEM)] + [vmem] * 7,
         out_specs=[vmem] * 4,
-        scratch_shapes=[half_map] * 2
-        + [full_map]
-        + [half_map] * 2
-        + [full_map]
-        + [half_map] * 2
+        scratch_shapes=[half_map] * 8
         + [
             full_map,
             pltpu.VMEM((lanes, 6 * lanes), jnp.float32),
@@ -441,7 +508,6 @@
         jnp.zeros((rows_dev + diags, 2 * channels), jnp.float32), own, me * sub, 0
     )
     conv_rows = conv_part.size // 128
-    features = embeddings.shape[0]
     scaling = 1.0 / math.sqrt(total_bins * diags)
     wide_both = (2 * channels, rows_dev + diags)
     diag_steps, bin_steps = n_diag.bit_length() - 1, n_bin.bit_length() - 1

time: 162 us -> 135 us (0.83)
  local copies, waits for them, and re-layouts: 39.6 us -> 24.6 us
  starting transfers between devices: 14.4 us -> 1.11 us
  Pallas kernels: 92.8 us -> 99.4 us
  other arithmetic: 11.7 us -> 8.59 us
    pallas_call x0 -> x1, Pallas kernels: none -> 16.9 us  [on_device(): pl.pallas_call(functools.partial(opening, (n_bin, n_diag, sub, span, cot_...]
    ppermute x5 -> x0, starting transfers between devices: 11.2 us -> none  [the longest x2 8.12 us: around(): lax.ppermute(block[:, rows_dev - before:], 'bin', shifted('bin', n_bin, 1))]
    dynamic_update_slice x2 -> x0, local copies, waits for them, and re-layouts: 8.36 us -> none  [on_device(): lax.dynamic_update_index_in_dim(cot, piece, lax.rem(me - k + n_diag, n_di...]
    pallas_call x1, Pallas kernels: 65.6 us -> 58.6 us  [on_device(): pl.pallas_call(functools.partial(kernel, (sub, groups, total_bins, n1, n2...]
    pallas_call x1, Pallas kernels: 27.2 us -> 23.9 us  [on_device(): pl.pallas_call(functools.partial(tail, (n_bin, n_diag, rows_dev, scaling)...]
    slice x1, local copies, waits for them, and re-layouts: 0.56 us -> 3.76 us  [on_device(): projected[d:d + reads, channels:]]
    reshape x1, local copies, waits for them, and re-layouts: 2.9 us -> 0.61 us  [on_device(): cot.reshape(groups, PACK, blocks, n2)]
    reshape x1, local copies, waits for them, and re-layouts: 2.97 us -> 0.78 us  [on_device(): jnp.transpose(pred.reshape(blocks, PACK, n2, groups), (3, 1, 0, 2))]
  transfers between devices with their start and end apart: 7 -> 1, of which waited for: 0 -> 0; matrix products, arithmetic and copies ran while one was open for 19% -> 4% of each run, Pallas kernels for 17% -> 18%
where the time goes in v4:
time: 135 us
  Pallas kernels  99.4 us (74%)
  local copies, waits for them, and re-layouts  24.6 us (18%)
  other arithmetic  8.59 us (6%)
    pallas_call x1, Pallas kernels, on_device(): pl.pallas_call(functools.partial(kernel, (sub, groups, total_bins, n1, n2...  58.6 us
    pallas_call x1, Pallas kernels, on_device(): pl.pallas_call(functools.partial(tail, (n_bin, n_diag, rows_dev, scaling)...  23.9 us
    pallas_call x1, Pallas kernels, on_device(): pl.pallas_call(functools.partial(opening, (n_bin, n_diag, sub, span, cot_...  16.9 us
    unnamed x38, local copies, waits for them, and re-layouts  7.14 us
    slice x1, local copies, waits for them, and re-layouts, on_device(): projected[d:d + reads, channels:]  3.76 us
    reshape x2, local copies, waits for them, and re-layouts, on_device(): pred.reshape(blocks, PACK, n2, groups)  2.94 us
  transfers between devices with their start and end apart: 1, of which 0 were waited for; matrix products, arithmetic and copies ran while one was open for 4% of the time, Pallas kernels for 18%

profile of v4, /device:TPU:0, one launch (start us, length us, event | category | flops | bytes accessed | tf_op | source)
XLA Modules:
  0.0 134.8 jit_solution(11387415510823634194)
XLA Ops:
  0.7 1.4 %copy.29.projection = bf16[128,64]{1,0:T(8,128)(2,1)} copy(bf16[128,64]{0,1:T(8,128)(2,1)} %param.9) | data formatting | bytes 32768 | tf_op args[1]
  2.1 1.7 %fusion.2.cot_in = f32[128,384]{1,0:T(8,128)} fusion(f32[128,384]{1,0:T(8,128)} %param.15, s32[384]{0:T(512)} %param.14, s32[384]{0:T(512)S(1)} %iota_add_fusion, s32[128]{0:T(128)S(1)} %iota_add_fusion.1), kind=kLoop, calls=%fused_computation.13 | loop fusion | flops 245760 | bytes 396800 | tf_op jit(solution)/shard_map/jit(_where)/select_n | solution.py:444
  3.8 16.9 %opening.1 = (f32[512,64]{1,0:T(8,128)}, f32[2,128,256]{2,1,0:T(8,128)}) custom-call(bf16[128,384]{1,0:T(8,128)(2,1)} %embeddings.3, bf16[128,64]{1,0:T(8,128)(2,1)} %copy.29.projection, f32[128,384]{1,0:T(8,128)} %fusion.2.cot_in), custom_call_target="tpu_custom_call" | custom-call | tf_op jit(solution)/shard_map/opening/pallas_call | solution.py:422
  20.7 3.8 %fusion.6 = (f32[472,32]{1,0:T(8,128)S(1)}, f32[472,32]{1,0:T(8,128)S(1)}, f32[472,32]{1,0:T(8,128)}, f32[472,32]{1,0:T(8,128)}, f32[472,32]{1,0:T(8,128)}, /*in...) fusion(f32[512,64]{1,0:T(8,128)} %get-tuple-element.13), kind=kLoop, calls=%fused_computation.29 | loop fusion | bytes 966656 | tf_op jit(solution)/shard_map/slice | solution.py:450
  24.5 0.9 slice.73
  25.4 0.1 copy.30
  25.5 0.1 copy.40
  25.6 0.8 copy.41
  26.4 0.6 reshape.71
  27.0 1.1 copy.34
  28.2 0.3 reshape.72
  28.6 0.9 fusion.8
  29.4 0.1 mul.89
  29.5 0.1 mul.93
  29.6 0.1 mul.86
  29.7 0.1 mul.87
  29.8 0.1 pad.56.clone
  29.8 0.6 pad_maximum_fusion.2.head
  30.4 0.7 maximum_maximum_fusion.1.expand
  31.1 0.9 copy.33
  32.0 0.7 reshape.70.bias
  32.7 0.4 maximum_bitcast_fusion
  33.2 0.8 pad_maximum_fusion.right
  34.0 0.7 pad_maximum_fusion.1.left
  34.7 0.9 maximum_maximum_fusion.cots
  35.6 0.6 pad_add_fusion.1.info
  36.3 58.6 %band.1 = (f32[13,8,512]{2,1,0:T(8,128)}, f32[6,32,256]{2,1,0:T(8,128)}, f32[2,440,128]{2,1,0:T(8,128)}, f32[2,9,32,32]{3,2,1,0:T(8,128)}) custom-call(s32[3]{0:T(128)} %pad_add_fusion.1.info, f32[2,224,128]{2,1,0:T(8,128)} %pad_maximum_fusion.1.left, f32[2,472,128]{2,1,0:T(8,128)} %pad_maximum_fusion.right, f32[32,256]{1,0:T(8,128)} %reshape.70.bias, ...), custom_call_target="tpu_custom_call" | custom-call | tf_op jit(solution)/shard_map/band/pallas_call | solution.py:478
  94.9 1.2 reshape.73
  96.1 1.8 %copy.35 = f32[13,8,16,32]{2,0,1,3:T(8,128)S(1)} copy(f32[13,8,16,32]{3,2,1,0:T(8,128)S(1)} %reshape.73) | data formatting | bytes 425984 | tf_op jit(solution)/shard_map/reshape | solution.py:543
  97.8 0.8 reshape.74
  98.6 0.1 slice.98
  98.8 1.1 collective-permute-start
  99.9 0.2 copy.37
  100.2 0.2 reshape.75
  100.5 0.2 reduce_sum.9
  100.7 0.1 copy.36
  100.8 0.3 copy-done.9
  101.1 0.8 reshape.76.conv_in
  101.8 0.2 pad_add_fusion
  102.1 0.8 dynamic_update_slice.11
  102.9 0.7 copy-done.6
  103.5 23.9 %tail.1 = (f32[128,384]{1,0:T(8,128)}, f32[64,128]{1,0:T(8,128)}, f32[144,128]{1,0:T(8,128)}) custom-call(f32[64,640]{1,0:T(8,128)} %bitcast.27, f32[144,128]{1,0:T(8,128)} %reshape.76.conv_in, bf16[128,384]{1,0:T(8,128)(2,1)} %embeddings.3, bf16[128,64]{1,0:T(8,128)(2,1)} %copy.29.projection), custom_call_target="tpu_custom_call" | custom-call | tf_op jit(solution)/shard_map/tail/pallas_call | solution.py:515
  127.5 1.7 %reshape.77 = f32[2,9,32,32]{3,2,1,0:T(8,128)} reshape(f32[144,128]{1,0:T(8,128)} %get-tuple-element.21) | data formatting | bytes 147456 | tf_op jit(solution)/shard_map/reshape | solution.py:541
  129.2 0.9 dynamic_update_slice.9
  130.1 0.9 dynamic_update_slice.10
  131.0 0.8 fusion.1
  131.8 1.6 %copy.47 = f32[128,384]{1,0:T(8,128)} copy(f32[128,384]{1,0:T(8,128)} %get-tuple-element.57) | data formatting | bytes 393216
  133.4 1.4 %copy.48 = f32[128,64]{0,1:T(8,128)} copy(f32[128,64]{0,1:T(8,128)} %bitcast.32) | data formatting | bytes 65536
  (48 shorter events, 0.3 us)
Async XLA Ops:
  0.6 20.0 %copy-start.13 = (s32[128]{0:T(128)}, s32[128]{0:T(128)S(1)}, u32[]{:S(2)}) copy-start(s32[128]{0:T(128)S(1)} %iota_add_fusion.1) | copy-start | bytes 1540
  20.7 5.7 %copy-start.10 = (f32[2,128,256]{2,1,0:T(8,128)S(1)}, f32[2,128,256]{2,1,0:T(8,128)}, u32[]{:S(2)}) copy-start(f32[2,128,256]{2,1,0:T(8,128)} %get-tuple-element.14) | copy-start | bytes 786436
  28.1 4.6 %copy-start = (f32[472,32]{1,0:T(8,128)S(1)}, f32[472,32]{1,0:T(8,128)}, u32[]{:S(2)}) copy-start(f32[472,32]{1,0:T(8,128)} %get-tuple-element.38) | copy-start | bytes 181252
  28.1 4.6 %copy-start.1 = (f32[472,32]{1,0:T(8,128)S(1)}, f32[472,32]{1,0:T(8,128)}, u32[]{:S(2)}) copy-start(f32[472,32]{1,0:T(8,128)} %get-tuple-element.39) | copy-start | bytes 181252
  28.1 4.6 %copy-start.2 = (f32[472,32]{1,0:T(8,128)S(1)}, f32[472,32]{1,0:T(8,128)}, u32[]{:S(2)}) copy-start(f32[472,32]{1,0:T(8,128)} %get-tuple-element.40) | copy-start | bytes 181252
  28.1 4.6 %copy-start.3 = (f32[472,32]{1,0:T(8,128)S(1)}, f32[472,32]{1,0:T(8,128)}, u32[]{:S(2)}) copy-start(f32[472,32]{1,0:T(8,128)} %get-tuple-element.41) | copy-start | bytes 181252
  28.1 4.6 %copy-start.4 = (f32[472,32]{1,0:T(8,128)S(1)}, f32[472,32]{1,0:T(8,128)}, u32[]{:S(2)}) copy-start(f32[472,32]{1,0:T(8,128)} %get-tuple-element.42) | copy-start | bytes 181252
  28.2 4.6 %copy-start.5 = (f32[472,32]{1,0:T(8,128)S(1)}, f32[472,32]{1,0:T(8,128)}, u32[]{:S(2)}) copy-start(f32[472,32]{1,0:T(8,128)} %get-tuple-element.43) | copy-start | bytes 181252
  28.5 5.5 %copy-start.7 = (f32[224,128]{1,0:T(8,128)S(1)}, f32[224,128]{1,0:T(8,128)}, u32[]{:S(2)}) copy-start(f32[224,128]{1,0:T(8,128)} %copy.41) | copy-start | bytes 344068
  32.7 2.9 %copy-start.15 = (s32[2]{0:T(128)S(1)}, s32[2]{0:T(128)}, u32[]{:S(2)}) copy-start(s32[2]{0:T(128)} %param.13) | copy-start | bytes 28
  97.8 2.1 %copy-start.8 = (f32[2,440,128]{2,1,0:T(8,128)S(1)}, f32[2,440,128]{2,1,0:T(8,128)}, u32[]{:S(2)}) copy-start(f32[2,440,128]{2,1,0:T(8,128)} %get-tuple-element.17) | copy-start | bytes 1351684
  98.6 1.6 %copy-start.11 = (f32[6,32,256]{2,1,0:T(8,128)S(1)}, f32[6,32,256]{2,1,0:T(8,128)}, u32[]{:S(2)}) copy-start(f32[6,32,256]{2,1,0:T(8,128)} %get-tuple-element.16) | copy-start | bytes 589828
  98.8 31.3 %collective-permute-start = (f32[128,192]{1,0:T(8,128)S(1)}, f32[128,192]{1,0:T(8,128)S(1)}, u32[]{:S(2)}, u32[]{:S(2)}) collective-permute-start(f32[128,192]{1,0:T(8,128)S(1)} %get-tuple-element.34), channel_id=1, source_target_pairs={{0,1},{1,0},{2,3},{3,2},{4,5},{5,4},{6,7},{7,6},{8,9},{9,8},{10,11... | collective-permute-start | bytes 294920 | tf_op jit(solution)/shard_map/ppermute | solution.py:551
  100.1 1.0 copy-start.9
  100.5 30.5 %copy-start.12 = (s32[384]{0:T(512)S(1)}, s32[384]{0:T(512)}, u32[]{:S(2)}) copy-start(s32[384]{0:T(512)} %param.14) | copy-start | bytes 4612
  100.5 30.5 %copy-start.14 = (s32[128]{0:T(128)S(1)}, s32[128]{0:T(128)}, u32[]{:S(2)}) copy-start(s32[128]{0:T(128)} %copy-done.13) | copy-start | bytes 1540
  102.9 0.7 copy-start.6

commit v5 on v4

--- a/solution.py
+++ b/solution.py
@@ -109,7 +109,7 @@
             halves = []
             for half in range(2):
                 partner = right[half, pl.ds(at, groups, stride=PACK), :]
-                halves.append(partner + left[half, pl.ds(at, 1), :])
+                halves.append(partner + left[pl.ds(at, 1), :])
             rows.append(jnp.concatenate(halves, axis=1) + bias[...])
         t = jnp.tanh(jnp.concatenate(rows, axis=0))
         keep = inside_rows(start, n0)
@@ -209,7 +209,7 @@
 
 
 def opening(
-    plan, embeddings, projection, cot_in, projected, cot_out,
+    plan, embeddings, projection, cot_in, left, right, cot_out,
     low, high, cot_low, cot_high, parts, part_slots, cots, cot_slots, send, recv,
 ):
     n_bin, n_diag, sub, span, cot_span = plan
@@ -283,7 +283,15 @@
     for k in range(1, n_diag):
         moves[k - 1].wait()
         total = total + part_slots[k - 1]
-    projected[...] = jnp.transpose(total)
+    channels = total.shape[0] // 2
+    left[...] = jnp.transpose(jnp.concatenate([total[:channels]] * (PACK // 2), axis=0))
+    turned = [
+        total[channels:] if d == 0 else pltpu.roll(total[channels:], total.shape[1] - d, 1)
+        for d in range(PACK)
+    ]
+    for h in range(2):
+        part = turned[h * PACK // 2 : (h + 1) * PACK // 2]
+        right[h] = jnp.transpose(jnp.concatenate(part, axis=0))
     cot_out[me_diag] = cots[me_diag]
     for k in range(1, n_diag):
         cot_moves[k - 1].wait()
@@ -295,7 +303,7 @@
 
 
 def tail(
-    plan, both_in, conv_in, embeddings, projection, embed_out, proj_out, conv_out,
+    plan, left_in, right_in, conv_in, embeddings, projection, embed_out, proj_out, conv_out,
     both, both_slots, conv_slots, spill_slot, sums, cut_slot, held, sum_slots, far_slot,
     send, recv,
 ):
@@ -317,6 +325,7 @@
     near = partners[len(diag_bits)]
     ids = iter(range(64))
     count, half = conv_in.shape[0], both.shape[0] // 2
+    sub, reach = left_in.shape[0], left_in.shape[0] + both.shape[1] - rows
 
     def copy(source, target, at, device):
         return pltpu.make_async_remote_copy(
@@ -324,7 +333,28 @@
             device_id=device, device_id_type=pl.DeviceIdType.MESH,
         )
 
-    both[...] = both_in[...]
+    both[...] = jnp.zeros_like(both)
+    fold = (
+        lax.broadcasted_iota(jnp.int32, (half, PACK * half), 0)
+        == lax.broadcasted_iota(jnp.int32, (half, PACK * half), 1) & (half - 1)
+    ).astype(jnp.float32)
+    lefts = lax.dot_general(
+        fold, left_in[...], (((1,), (1,)), ((), ())),
+        precision=HIGHEST, preferred_element_type=jnp.float32,
+    )
+    rights = jnp.zeros((half, right_in.shape[1]), jnp.float32)
+    for h in range(2):
+        turned = jnp.transpose(right_in[h])
+        for q in range(PACK // 2):
+            d = h * PACK // 2 + q
+            piece = turned[q * half : (q + 1) * half]
+            rights = rights + (pltpu.roll(piece, d, 1) if d else piece)
+    for d in range(n_diag):
+        @pl.when(me_diag == d)
+        def _():
+            both[:half, d * sub : (d + 1) * sub] = lefts
+            both[half:, d * sub : d * sub + reach] = rights[:, :reach]
+
     sums[:count] = conv_in[...]
     mine, theirs = me_bin % 2, 1 - me_bin % 2
     conv_half, proj_half = count // 2, half
@@ -419,14 +449,15 @@
     wide_span, wide_cot = -(-span // 128) * 128, -(-cot_span // 128) * 128
     features = embeddings.shape[0]
     vmem = pl.BlockSpec(memory_space=pltpu.VMEM)
-    projected, cot = pl.pallas_call(
+    left, right, cot = pl.pallas_call(
         functools.partial(opening, (n_bin, n_diag, sub, span, cot_span)),
         out_shape=[
-            jax.ShapeDtypeStruct((wide_span, 2 * channels), jnp.float32),
+            jax.ShapeDtypeStruct((wide_span, lanes // 2), jnp.float32),
+            jax.ShapeDtypeStruct((2, wide_span, lanes // 2), jnp.float32),
             jax.ShapeDtypeStruct((n_diag, diag_dev, wide_cot), jnp.float32),
         ],
         in_specs=[vmem] * 3,
-        out_specs=[vmem] * 2,
+        out_specs=[vmem] * 3,
         scratch_shapes=[
             pltpu.VMEM((features, 128), jnp.bfloat16),
             pltpu.VMEM((features, rows_dev), jnp.bfloat16),
@@ -444,12 +475,6 @@
     )(embeddings, projection, jnp.where(counted, cotangent, 0.0))
     cot = cot[:, :, :cot_span]
     region = sub + 2 * HALO
-    reads = region + PACK * (groups - 1)
-    left = jnp.tile(projected[:region, :channels], (1, PACK))
-    right = jnp.concatenate(
-        [projected[d : d + reads, channels:] for d in range(PACK)], axis=1
-    )
-    halves = lambda x: jnp.stack([x[:, : lanes // 2], x[:, lanes // 2 :]])
     bias = jnp.transpose(dist_bias.reshape(channels, groups, PACK), (1, 2, 0)).reshape(
         groups, lanes
     )
@@ -472,7 +497,7 @@
     head = jnp.concatenate([spread(head_high), spread(head_low)])
     info = jnp.concatenate([dilations, (first_row + me * sub - HALO)[None].astype(jnp.int32)])
 
-    writes = sub + PACK * (groups - 1)
+    writes = -(-(sub + diags) // 128) * 128
     full_map = pltpu.VMEM((region, groups, lanes), jnp.float32)
     half_map = pltpu.VMEM((region, groups, lanes), jnp.bfloat16)
     pred, grad_left, grad_right, conv_part = pl.pallas_call(
@@ -493,20 +518,8 @@
         ],
         compiler_params=pltpu.CompilerParams(vmem_limit_bytes=60 * 1024 * 1024),
         name="band",
-    )(info, halves(left), halves(right), bias, conv_weight, expand, head, cots)
-
-    grad_right = jnp.concatenate([grad_right[0], grad_right[1]], axis=1)
-    spilled = jnp.zeros((sub + diags, channels), jnp.float32)
-    for d in range(PACK):
-        spilled = spilled + jnp.pad(
-            grad_right[:, d * channels : (d + 1) * channels],
-            ((d, sub + diags - writes - d), (0, 0)),
-        )
-    lefts = jnp.sum(grad_left.reshape(sub, PACK, channels), axis=1)
-    own = jnp.concatenate([jnp.pad(lefts, ((0, diags), (0, 0))), spilled], axis=1)
-    buffer = lax.dynamic_update_slice_in_dim(
-        jnp.zeros((rows_dev + diags, 2 * channels), jnp.float32), own, me * sub, 0
-    )
+    )(info, left, right, bias, conv_weight, expand, head, cots)
+
     conv_rows = conv_part.size // 128
     scaling = 1.0 / math.sqrt(total_bins * diags)
     wide_both = (2 * channels, rows_dev + diags)
@@ -519,7 +532,7 @@
             jax.ShapeDtypeStruct((2 * channels, features), jnp.float32),
             jax.ShapeDtypeStruct((conv_rows, 128), jnp.float32),
         ],
-        in_specs=[vmem] * 4,
+        in_specs=[vmem] * 5,
         out_specs=[vmem] * 3,
         scratch_shapes=[
             pltpu.VMEM(wide_both, jnp.float32),
@@ -536,22 +549,29 @@
         ],
         compiler_params=pltpu.CompilerParams(collective_id=0, has_side_effects=True),
         name="tail",
-    )(jnp.transpose(buffer), conv_part.reshape(conv_rows, 128), embeddings, projection)
+    )(
+        grad_left.reshape(sub, lanes), grad_right, conv_part.reshape(conv_rows, 128),
+        embeddings, projection,
+    )
     grad_proj = jnp.transpose(proj_sum)
     grad_conv = conv_sum.reshape(conv_part.shape)
 
     pred = jnp.transpose(pred.reshape(blocks, PACK, n2, groups), (3, 1, 0, 2)).reshape(
         diags, cot_span
     )[:, margin : margin + sub]
-    pred_local = jnp.zeros((diag_dev, rows_dev), jnp.float32)
+    pieces = []
     for k in range(n_diag):
         other = lax.rem(me + k, n_diag)
         piece = lax.dynamic_slice_in_dim(pred, other * diag_dev, diag_dev, 0)
-        if k:
-            piece = lax.ppermute(piece, "diag", pairs(k))
-        pred_local = lax.dynamic_update_slice_in_dim(
-            pred_local, piece, lax.rem(me - k + n_diag, n_diag) * sub, 1
-        )
+        pieces.append(lax.ppermute(piece, "diag", pairs(k)) if k else piece)
+    columns = []
+    for d in range(n_diag):
+        source = lax.rem(me - d + n_diag, n_diag)
+        chosen = pieces[0]
+        for k in range(1, n_diag):
+            chosen = jnp.where(source == k, pieces[k], chosen)
+        columns.append(chosen)
+    pred_local = jnp.concatenate(columns, axis=1)
     pred_local = jnp.where(counted, pred_local, 0.0)
     return (pred_local, grad_embed, grad_proj, grad_conv)
 

time: 135 us -> 123 us (0.911)
  local copies, waits for them, and re-layouts: 24.6 us -> 15.2 us
  other arithmetic: 8.59 us -> 5.31 us
    slice x6 -> x0, local copies, waits for them, and re-layouts: 4.79 us -> none  [the longest x1 3.76 us: on_device(): projected[d:d + reads, channels:]]
    unnamed x38 -> x14, local copies, waits for them, and re-layouts: 7.14 us -> 4.55 us
    dynamic_update_slice x3 -> x0, local copies, waits for them, and re-layouts: 2.52 us -> none  [the longest x2 1.73 us: on_device(): lax.dynamic_update_slice_in_dim(pred_local, piece, lax.rem(me - k + n_dia...]
    another operation x3 -> x0, other arithmetic: 1.98 us -> none  [on_device(): halves = lambda x: jnp.stack([x[:, :lanes // 2], x[:, lanes // 2:]])]
  transfers between devices with their start and end apart: 1 -> 1, of which waited for: 0 -> 0; matrix products, arithmetic and copies ran while one was open for 4% -> 2% of each run, Pallas kernels for 18% -> 20%
where the time goes in v5:
time: 123 us
  Pallas kernels  100 us (81%)
  local copies, waits for them, and re-layouts  15.2 us (12%)
  other arithmetic  5.31 us (4%)
    pallas_call x1, Pallas kernels, on_device(): pl.pallas_call(functools.partial(kernel, (sub, groups, total_bins, n1, n2...  58.6 us
    pallas_call x1, Pallas kernels, on_device(): pl.pallas_call(functools.partial(tail, (n_bin, n_diag, rows_dev, scaling)...  24.4 us
    pallas_call x1, Pallas kernels, on_device(): pl.pallas_call(functools.partial(opening, (n_bin, n_diag, sub, span, cot_...  17 us
    unnamed x14, local copies, waits for them, and re-layouts  4.55 us
    reshape x2, local copies, waits for them, and re-layouts, on_device(): pred.reshape(blocks, PACK, n2, groups)  2.94 us
  transfers between devices with their start and end apart: 1, of which 0 were waited for; matrix products, arithmetic and copies ran while one was open for 2% of the time, Pallas kernels for 20%

profile of v5, /device:TPU:0, one launch (start us, length us, event | category | flops | bytes accessed | tf_op | source)
XLA Modules:
  0.0 122.5 jit_solution(15144868094563925658)
XLA Ops:
  0.7 1.4 %copy.17.projection = bf16[128,64]{1,0:T(8,128)(2,1)} copy(bf16[128,64]{0,1:T(8,128)(2,1)} %param.9) | data formatting | bytes 32768 | tf_op args[1]
  2.1 1.7 %fusion.1.cot_in = f32[128,384]{1,0:T(8,128)} fusion(f32[128,384]{1,0:T(8,128)} %param.15, s32[384]{0:T(512)} %param.14, s32[384]{0:T(512)S(1)} %iota_add_fusion, s32[128]{0:T(128)S(1)} %iota_add_fusion.1), kind=kLoop, calls=%fused_computation.7 | loop fusion | flops 245760 | bytes 396800 | tf_op jit(solution)/shard_map/jit(_where)/select_n | solution.py:475
  3.8 17.0 %opening.1 = (f32[512,128]{1,0:T(8,128)}, f32[2,512,128]{2,1,0:T(8,128)}, f32[2,128,256]{2,1,0:T(8,128)}) custom-call(bf16[128,384]{1,0:T(8,128)(2,1)} %embeddings.3, bf16[128,64]{1,0:T(8,128)(2,1)} %copy.17.projection, f32[128,384]{1,0:T(8,128)} %fusion.1.cot_in), custom_call_target="tpu_custom_call" | custom-call | tf_op jit(solution)/shard_map/opening/pallas_call | solution.py:452
  20.9 1.7 %reshape.67 = f32[32,8,13,16]{3,2,1,0:T(8,128)S(1)} reshape(f32[2,128,208]{2,1,0:T(8,128)} %bitcast.16) | data formatting | bytes 425984 | tf_op jit(solution)/shard_map/reshape | solution.py:487
  22.5 0.0 copy-start.3
  22.5 0.0 copy-start.1
  22.6 0.0 copy-start.4
  22.6 1.1 copy.19
  23.7 0.3 reshape.68
  24.1 0.0 copy-done.3
  24.1 0.1 mul.82
  24.2 0.1 mul.86
  24.3 0.1 mul.39
  24.4 0.1 mul.80
  24.5 0.1 pad.11.clone
  24.5 0.6 pad_maximum_fusion.head
  25.1 0.7 maximum_maximum_fusion.1.expand
  25.8 0.0 copy-done.1
  25.8 0.1 copy.18
  25.9 0.7 reshape.66.bias
  26.6 0.9 maximum_maximum_fusion.cots
  27.5 0.0 copy-done.4
  27.5 0.6 pad_add_fusion.info
  28.1 58.6 %band.1 = (f32[13,8,512]{2,1,0:T(8,128)}, f32[6,32,256]{2,1,0:T(8,128)}, f32[2,512,128]{2,1,0:T(8,128)}, f32[2,9,32,32]{3,2,1,0:T(8,128)}) custom-call(s32[3]{0:T(128)} %pad_add_fusion.info, f32[512,128]{1,0:T(8,128)} %get-tuple-element.14.left, f32[2,512,128]{2,1,0:T(8,128)} %get-tuple-element.15.right, f32[32,256]{1,0:T(8,128)} %reshape.66.bias, ...), custom_call_target="tpu_custom_call" | custom-call | tf_op jit(solution)/shard_map/band/pallas_call | solution.py:503
  86.7 1.2 reshape.69
  87.9 1.8 %copy.20 = f32[13,8,16,32]{2,0,1,3:T(8,128)S(1)} copy(f32[13,8,16,32]{3,2,1,0:T(8,128)S(1)} %reshape.69) | data formatting | bytes 425984 | tf_op jit(solution)/shard_map/reshape | solution.py:559
  89.7 0.0 copy-start
  89.7 0.8 reshape.70
  90.5 0.0 copy-start.2
  90.5 0.1 slice.8
  90.6 1.1 collective-permute-start
  91.7 0.0 copy-done
  91.7 0.8 reshape.72.conv_in
  92.5 24.4 %tail.1 = (f32[128,384]{1,0:T(8,128)}, f32[64,128]{1,0:T(8,128)}, f32[144,128]{1,0:T(8,128)}) custom-call(f32[192,256]{1,0:T(8,128)} %bitcast.17, f32[2,512,128]{2,1,0:T(8,128)} %get-tuple-element.19.right_in, f32[144,128]{1,0:T(8,128)} %reshape.72.conv_in, bf16[128,384]{1,0:T(8,128)(2,1)} %embeddings.3, bf16[128,64]{1,0:T(8,128)(2,1)} %copy.17.projection), custom_call_target="tpu_custom_call" | custom-call | tf_op jit(solution)/shard_map/tail/pallas_call | solution.py:528
  116.9 1.7 %reshape.73 = f32[2,9,32,32]{3,2,1,0:T(8,128)} reshape(f32[144,128]{1,0:T(8,128)} %get-tuple-element.23) | data formatting | bytes 147456 | tf_op jit(solution)/shard_map/reshape | solution.py:557
  118.7 0.0 collective-permute-done
  118.7 0.0 copy-done.2
  118.7 0.8 maximum_select_fusion
  119.5 1.6 %copy.24 = f32[128,384]{1,0:T(8,128)} copy(f32[128,384]{1,0:T(8,128)} %get-tuple-element.37) | data formatting | bytes 393216
  121.1 1.4 %copy.25 = f32[128,64]{0,1:T(8,128)} copy(f32[128,64]{0,1:T(8,128)} %bitcast.18) | data formatting | bytes 65536
  (11 shorter events, 0.1 us)
Async XLA Ops:
  22.5 1.6 %copy-start.3 = (f32[32]{0:T(128)S(1)}, f32[32]{0:T(128)}, u32[]{:S(2)}) copy-start(f32[32]{0:T(128)} %param.12) | copy-start | bytes 388
  22.5 3.3 %copy-start.1 = (f32[32,256]{1,0:T(8,128)S(1)}, f32[32,256]{1,0:T(8,128)}, u32[]{:S(2)}) copy-start(f32[32,256]{1,0:T(8,128)} %param.10) | copy-start | bytes 98308
  22.6 5.0 %copy-start.4 = (s32[2]{0:T(128)S(1)}, s32[2]{0:T(128)}, u32[]{:S(2)}) copy-start(s32[2]{0:T(128)} %param.13) | copy-start | bytes 28
  89.7 2.1 %copy-start = (f32[2,9,32,32]{3,2,1,0:T(8,128)S(1)}, f32[2,9,32,32]{3,2,1,0:T(8,128)}, u32[]{:S(2)}) copy-start(f32[2,9,32,32]{3,2,1,0:T(8,128)} %get-tuple-element.20) | copy-start | bytes 221188
  90.5 28.3 %copy-start.2 = (s32[384]{0:T(512)S(1)}, s32[384]{0:T(512)}, u32[]{:S(2)}) copy-start(s32[384]{0:T(512)} %param.14) | copy-start | bytes 4612
  90.6 28.1 %collective-permute-start = (f32[128,192]{1,0:T(8,128)S(1)}, f32[128,192]{1,0:T(8,128)S(1)}, u32[]{:S(2)}, u32[]{:S(2)}) collective-permute-start(f32[128,192]{1,0:T(8,128)S(1)} %constant_dynamic-slice_fusion), channel_id=1, source_target_pairs={{0,1},{1,0},{2,3},{3,2},{4,5},{5,4},{6,7},{7,6},{8,9},{9,8},{10,11... | collective-permute-start | bytes 294920 | tf_op jit(solution)/shard_map/ppermute | solution.py:566
